TPU v7x, 32 devices: a whole 2x2x4 slice. The times are simulated.
32 devices in a mesh: node: 2 (over y), gz: 16 (over z, x, core).
Axes of the slice: x: 2, y: 2, z: 4, core: 2. Of those that a mesh axis runs over, the one named last changes fastest.
Arguments:
- source: float32 [2, 64, 512, 256], P(None, ('node', 'gz')), parts along dimension 1, may hold values from -56 to 56
- layer_ids: int32 [64, 256], P(('node', 'gz')), parts along dimension 0, may hold values from 0 to 15
- conduct_table: float32 [16], replicated, may hold values from 0.35 to 3.75
- shift: float32 [4], P('node'), parts along dimension 0, may hold values from 0.2 to 1
Outputs:
- solution_field: float32 [2, 64, 512, 256], P(None, ('node', 'gz')), parts along dimension 1
- residual_norms: float32 [4], P('node'), parts along dimension 0
There are 2 independent parts, one for each index of `node`. A program takes and returns all parts, laid end to end along the dimension named above; an argument that names none is the same for every part. Nothing has to cross between parts.
All inputs are finite; a program needn't handle non-finite values.
Results may differ from a plain program's by a relative error of at most 0.0003.
Values sent between devices are 32-bit elements; how exact they have to be, the bound alone decides.
No kernel may reach another device: no remote copies, remote signals or barrier semaphores. Data moves between devices by JAX's collectives and lax.ppermute only.
A program may use at most 64 MiB of HBM per device.

v0:
```python
import functools

import jax
import jax.numpy as jnp
import ml_dtypes
import numpy as np
from jax import lax
from jax.experimental import pallas as pl
from jax.experimental.pallas import tpu as pltpu
from jax.sharding import PartitionSpec as P

RADIX = 4
HALVES = 2
GROUP = RADIX * HALVES
CHUNKS = 2
SENDS = ((6, 7, 2, 3, 4, 0), (2, 6, 7, 3, 4, 5, 1, 0))
ANSWERS = tuple((t, d) for t in range(CHUNKS) for d in SENDS[t])
JOINT = (5, 1)
TAG = 8

relax = 0.6


def sine_table(length):
    indices = np.arange(1, length + 1)
    product = indices[:, None] * indices[None, :] % (2 * (length + 1))
    return np.sqrt(2.0 / (length + 1)) * np.sin(np.pi / (length + 1) * product)


def sine_eigen(length):
    indices = np.arange(1, length + 1)
    return 4.0 * np.sin(np.pi / (2 * (length + 1)) * indices) ** 2


def wave_numbers(length):
    return RADIX * np.arange(length // RADIX)[None, :] + np.arange(RADIX)[:, None]


def wave_eigen(length):
    return 4.0 * np.sin(np.pi / length * wave_numbers(length)) ** 2


def wave_tables(length):
    waves = wave_numbers(length)
    short = length // RADIX
    product = waves[:, :, None] * np.arange(short)[None, None, :] % length
    angles = 2.0 * np.pi / length * product
    cos_t, sin_t = np.cos(angles), np.sin(angles)
    pieces = HALVES * CHUNKS
    top = np.concatenate([cos_t, sin_t], axis=2).reshape(RADIX, pieces, short // pieces, 2 * short)
    low = np.concatenate([-sin_t, cos_t], axis=2).reshape(RADIX, pieces, short // pieces, 2 * short)
    return np.concatenate([top, low], axis=2).reshape(RADIX, 2 * short, 2 * short)


def two_terms(table):
    first = table.astype(ml_dtypes.bfloat16)
    return np.stack([first, (table - first.astype(np.float64)).astype(ml_dtypes.bfloat16)])


def split(value):
    first = value.astype(jnp.bfloat16)
    return first, (value - first.astype(jnp.float32)).astype(jnp.bfloat16)


def dot_right(value, table):
    rows = value.shape[0]
    first, second = split(value)
    wide = jnp.dot(jnp.concatenate([first, second], axis=0), table[0], preferred_element_type=jnp.float32)
    return wide[:rows] + (wide[rows:] + jnp.dot(first, table[1], preferred_element_type=jnp.float32))


def dot_left(table, value):
    rows = table.shape[0] // 2
    first, second = split(value)
    wide = jnp.dot(table, first, preferred_element_type=jnp.float32)
    return wide[:rows] + (wide[rows:] + jnp.dot(table[:rows], second, preferred_element_type=jnp.float32))


def cmul(a, b):
    return (a[0] * b[0] - a[1] * b[1], a[0] * b[1] + a[1] * b[0])


def csqr(a):
    cross = a[0] * a[1]
    return ((a[0] - a[1]) * (a[0] + a[1]), cross + cross)


def cpow(a, count):
    result = None
    while count:
        if count & 1:
            result = a if result is None else cmul(result, a)
        count >>= 1
        if count:
            a = csqr(a)
    return result


def cadd(a, b):
    return (a[0] + b[0], a[1] + b[1])


def csub(a, b):
    return (a[0] - b[0], a[1] - b[1])


def cscale(a, scale):
    return (a[0] * scale, a[1] * scale)


def cmore(total, factor, term):
    return cadd(total, cmul(factor, term))


def cinv(a):
    scale = 1.0 / (a[0] * a[0] + a[1] * a[1])
    return (a[0] * scale, -a[1] * scale)


def cone(a):
    return (1.0 - a[0], -a[1])


def cpick(cond, a, b):
    return (jnp.where(cond, a[0], b[0]), jnp.where(cond, a[1], b[1]))


def rows_at(start, rows):
    if isinstance(start, int):
        return pl.ds(start, rows)
    return pl.ds(pl.multiple_of(start, 8), rows)


def load(ref, base, short, row, rows):
    return (ref[rows_at(base + row, rows), :], ref[rows_at(base + short + row, rows), :])


def store(ref, base, short, row, rows, value):
    ref[rows_at(base + row, rows), :] = value[0]
    ref[rows_at(base + short + row, rows), :] = value[1]


def each_strip(count, rows, body):
    def step(i, carry):
        body(pl.multiple_of(i * rows, rows))
        return carry

    steps = count // rows
    lax.fori_loop(0, steps, step, 0, unroll=min(steps, 4))


def squares_of(a):
    return a[0] * a[0] + a[1] * a[1]


def conduct_kernel(table_ref, ids_ref, out_ref):
    planes = ids_ref.shape[0]
    ids = ids_ref[...]
    cells = jnp.zeros(ids.shape, jnp.float32)
    for layer in range(table_ref.shape[0]):
        cells = jnp.where(ids == layer, table_ref[layer], cells)
    out_ref[...] = jnp.zeros_like(out_ref)
    out_ref[pl.ds(0, planes), :] = cells
    out_ref[pl.ds(TAG - 1, 1), :] = jnp.sum(cells, axis=0, keepdims=True)


def add_kernel(one_ref, two_ref, out_ref):
    out_ref[...] = one_ref[...] + two_ref[...]


def fill_tag(out_ref, planes, own_ref, below_ref, above_ref, *part_refs):
    start = out_ref.shape[0] - TAG
    for n, ref in enumerate((own_ref, below_ref, above_ref)):
        out_ref[pl.ds(start + n * planes, planes), :] = ref[pl.ds(0, planes), :]
    total = part_refs[0][pl.ds(TAG - 1, 1), :]
    for ref in part_refs[1:]:
        total = total + ref[pl.ds(TAG - 1, 1), :]
    out_ref[pl.ds(start + TAG - 1, 1), :] = total


def tag_of(ref):
    return ref[pl.ds(ref.shape[0] - TAG, TAG), :]


def find_numbers(cells_total, shift_ref, part_refs, numbers_ref):
    total = None
    for ref in part_refs:
        row = ref[pl.ds(ref.shape[0] - 1, 1), :]
        total = row if total is None else total + row
    inv = (1.0 / (jnp.sum(total, axis=1, keepdims=True) * (1.0 / cells_total)))[0, 0]
    numbers_ref[0] = shift_ref[0] * inv
    numbers_ref[1] = shift_ref[1] * inv
    numbers_ref[2] = relax * inv
    numbers_ref[3] = 0.5 * relax * inv
    numbers_ref[4] = shift_ref[0]
    numbers_ref[5] = shift_ref[1]


def faces_kernel(planes, blocks, flags_ref, *refs):
    part_refs, (faces_ref, padded_ref, below_ref, above_ref) = refs[:GROUP], refs[GROUP:]
    z, member = flags_ref[2], flags_ref[3]
    _, count, width = faces_ref.shape
    for d, ref in enumerate(part_refs):
        tag = tag_of(ref)
        place = member ^ d
        for p in range(planes):
            padded_ref[pl.ds(8 + place * planes + p, 1), :] = tag[p : p + 1]
        below_ref[pl.ds(place, 1), :] = tag[2 * planes - 1 : 2 * planes]
        above_ref[pl.ds(place, 1), :] = tag[2 * planes : 2 * planes + 1]
    cells = padded_ref[pl.ds(8, count), :]
    padded_ref[pl.ds(7, 1), :] = jnp.where(z == 0, cells[0:1], below_ref[pl.ds(GROUP - 1, 1), :])
    padded_ref[pl.ds(8 + count, 1), :] = jnp.where(
        z == blocks - 1, cells[count - 1 : count], above_ref[pl.ds(0, 1), :]
    )
    lane = lax.broadcasted_iota(jnp.int32, cells.shape, 1)
    last, first = lane == width - 1, lane == 0
    right = 0.5 * (cells + pltpu.roll(cells, width - 1, 1))
    left = 0.5 * (cells + pltpu.roll(cells, 1, 1))
    low = 0.5 * (cells + padded_ref[pl.ds(7, count), :])
    high = 0.5 * (cells + padded_ref[pl.ds(9, count), :])
    faces_ref[0] = jnp.where(last, cells, right) + jnp.where(first, cells, left) + (low + high)
    faces_ref[1] = cells
    faces_ref[2] = jnp.where(last, 0.0, right)
    faces_ref[3] = jnp.where(first, 0.0, left)
    faces_ref[4] = low
    faces_ref[5] = high


def forward_kernel(distance, tags_count, flags_ref, source_ref, wave_ref, *refs):
    tag_refs, out_refs, stage_ref = refs[:tags_count], refs[tags_count:-1], refs[-1]
    planes = source_ref.shape[1]
    q = flags_ref[0] ^ distance
    sign = (1 - 2 * (q & 1)).astype(jnp.float32)
    turn_re = jnp.where(q == 0, 1.0, jnp.where(q == 2, -1.0, 0.0))
    turn_im = jnp.where(q == 1, 1.0, jnp.where(q == 3, -1.0, 0.0))
    rows = stage_ref.shape[1] // (HALVES * CHUNKS)
    for p in range(planes):
        parts = [[source_ref[c, p, i] for i in range(RADIX)] for c in range(2)]
        even = [parts[c][0] + sign * parts[c][2] for c in range(2)]
        odd = [parts[c][1] + sign * parts[c][3] for c in range(2)]
        mixed = jnp.concatenate(
            [
                even[0] + (turn_re * odd[0] + turn_im * odd[1]),
                even[1] + (turn_re * odd[1] - turn_im * odd[0]),
            ],
            axis=0,
        )
        stage_ref[p] = dot_left(wave_ref[q], mixed)
        for n in range(HALVES):
            h = flags_ref[1] ^ n
            for t in range(CHUNKS):
                out_refs[n * CHUNKS + t][pl.ds(p * rows, rows), :] = stage_ref[
                    p, rows_at((h * CHUNKS + t) * rows, rows), :
                ]
    for ref in out_refs if tags_count else ():
        fill_tag(ref, planes, *tag_refs)


def tagged_kernel(planes, count, *refs):
    for ref, out_ref in zip(refs[:count], refs[-count:]):
        rows = ref.shape[0] - TAG
        out_ref[pl.ds(0, rows), :] = ref[pl.ds(0, rows), :]
        fill_tag(out_ref, planes, *refs[count:-count])


def backward_kernel(planes, cells, flags_ref, wave_ref, *refs):
    arrays, (out_ref, norms_ref, mixed_ref, stage_ref) = refs[:-4], refs[-4:]
    rows = (arrays[0].shape[0] - TAG) // planes
    came = {}
    for (t, d), ref in zip(ANSWERS, arrays):
        for n in range(CHUNKS if d in JOINT else 1):
            came[d, n if d in JOINT else t] = ref.at[pl.ds(n * planes * rows, planes * rows)]
    short = rows * CHUNKS * HALVES // 2
    total = None
    for ref in arrays:
        tag = tag_of(ref)
        total = tag if total is None else total + tag
    for d in range(RADIX):
        q = flags_ref[0] ^ d
        for p in range(planes):
            for n in range(HALVES):
                h = flags_ref[1] ^ n
                for t in range(CHUNKS):
                    stage_ref[d, p, rows_at((h * CHUNKS + t) * rows, rows), :] = came[d + RADIX * n, t][
                        pl.ds(p * rows, rows), :
                    ]
            mixed_ref[p, q] = dot_left(wave_ref[q], stage_ref[d, p])
    for p in range(planes):

        def strip(row):
            zero, one, two, three = [load(mixed_ref.at[p, q], 0, short, row, 8) for q in range(RADIX)]
            even, odd = cadd(zero, two), cadd(one, three)
            even_d, odd_d = csub(zero, two), csub(one, three)
            parts = (
                cadd(even, odd),
                (even_d[0] - odd_d[1], even_d[1] + odd_d[0]),
                csub(even, odd),
                (even_d[0] + odd_d[1], even_d[1] - odd_d[0]),
            )
            for i in range(RADIX):
                for c in range(2):
                    out_ref[c, p, rows_at(i * short + row, 8), :] = parts[i][c]

        each_strip(short, 8, strip)
    norms = jnp.sqrt(jnp.sum(total, axis=1, keepdims=True) * (1.0 / cells))
    for n in range(norms_ref.shape[0]):
        norms_ref[n] = norms[n, 0]


def decay_root(h):
    sq = (h[0] + 0.25 * (h[0] * h[0] - h[1] * h[1]), h[1] + 0.5 * h[0] * h[1])
    size = jnp.sqrt(squares_of(sq))
    root_re = jnp.sqrt(0.5 * (size + sq[0]))
    root = (root_re, 0.5 * sq[1] / root_re)
    return cinv((1.0 + 0.5 * h[0] + root[0], 0.5 * h[1] + root[1])), root


def two_powers(power, z, stacks):
    low = high = None
    bit = 0
    while (1 << bit) < stacks:
        taken = ((z >> bit) & 1) == 1
        if low is None:
            one = (jnp.ones_like(power[0]), jnp.zeros_like(power[0]))
            low, high = cpick(taken, power, one), cpick(taken, one, power)
        else:
            grown = cmul(cpick(taken, low, high), power)
            low, high = cpick(taken, grown, low), cpick(taken, high, grown)
        power = csqr(power)
        bit += 1
    return low, high


def sums_of(planes, rho, cross_f, cross_b):
    ahead = planes[0]
    for a in planes[1:]:
        ahead = cmore(a, rho, ahead)
    behind = planes[-1]
    for a in planes[-2::-1]:
        behind = cmore(a, rho, behind)
    return csub(ahead, cmul(cross_f, behind)), csub(behind, cmul(cross_b, ahead))


def sine_rows(source_ref, target_ref, sine_ref, count):
    sine = (sine_ref[0], sine_ref[1])
    rows = max(n for n in range(16, 641, 16) if count % n == 0)
    for i in range(0, count, rows):
        target_ref[pl.ds(i, rows), :] = dot_right(source_ref[pl.ds(i, rows), :], sine)


def fill_give(z, rows, sums_ref, give_refs):
    for ref in give_refs:
        ref[pl.ds(0, rows), :] = sums_ref[rows_at((z & 1) * rows, rows), :]
        ref[pl.ds(rows, TAG), :] = sums_ref[pl.ds(2 * rows, TAG), :]


def start_kernel(
    chunk, planes, blocks, cells_total, flags_ref, numbers_ref, wave_eig_ref, sine_eig_ref, sine_ref, *refs,
):
    part_refs, (field_ref, modes_ref, base_ref, sums_ref), give_refs = refs[:GROUP], refs[GROUP : GROUP + 4], refs[GROUP + 4 :]
    if chunk == 0:
        shift_ref, numbers_ref, give_refs = numbers_ref, give_refs[-1], give_refs[:-1]
        find_numbers(cells_total, shift_ref, part_refs, numbers_ref)
    q, h, z, member = [flags_ref[n] for n in range(4)]
    rows = base_ref.shape[1]
    part = rows * planes
    short = rows // 2
    count = GROUP * planes
    first_row = (h * CHUNKS + chunk) * short
    for d, ref in enumerate(part_refs):
        field_ref[rows_at((member ^ d) * part, part), :] = ref[pl.ds(0, part), :]
    sine_rows(field_ref, modes_ref, sine_ref, count * rows)
    h_re, h_im = numbers_ref[0], numbers_ref[1]
    sine_eig = sine_eig_ref[...]

    def strip(i, total):
        row = pl.multiple_of(i * 8, 8)
        eigen = wave_eig_ref[q, rows_at(first_row + row, 8), :] + sine_eig
        rho, _ = decay_root((eigen + h_re, jnp.full_like(eigen, h_im)))
        block = cpow(rho, count)
        next_one = cmul(block, rho)
        low, high = two_powers(csqr(block), z, blocks)
        cross_f, cross_b = cmul(next_one, low), cmul(next_one, high)
        for n, value in enumerate((rho, cross_f, cross_b, block, low, high)):
            store(base_ref.at[n], 0, short, row, 8, value)
        found = [load(modes_ref, l * rows, short, row, 8) for l in range(count)]
        ahead, behind = sums_of(found, rho, cross_f, cross_b)
        store(sums_ref, 0, short, row, 8, ahead)
        store(sums_ref, rows, short, row, 8, behind)
        for l in range(count):
            total = total + squares_of(load(field_ref, l * rows, short, row, 8))
        return total

    total = lax.fori_loop(
        0, short // 8, strip, jnp.zeros((8, field_ref.shape[1]), jnp.float32), unroll=2
    )
    sums_ref[pl.ds(2 * rows, TAG), :] = jnp.zeros((TAG, field_ref.shape[1]), jnp.float32)
    sums_ref[pl.ds(2 * rows, 1), :] = jnp.sum(total, axis=0, keepdims=True)
    fill_give(z, rows, sums_ref, give_refs)


def factors_kernel(
    chunk, count, levels, flags_ref, numbers_ref, wave_eig_ref, sine_eig_ref, base_ref, out_ref,
):
    q, h_part, z = flags_ref[0], flags_ref[1], flags_ref[2]
    short = base_ref.shape[1] // 2
    h_re, h_im, scale = numbers_ref[0], numbers_ref[1], numbers_ref[3]
    sine_eig = sine_eig_ref[...]

    def strip(row):
        eigen = wave_eig_ref[q, rows_at((h_part * CHUNKS + chunk) * short + row, 8), :] + sine_eig
        h = (eigen + h_re, jnp.full_like(eigen, h_im))
        rho, _, _, block, low, high = [load(base_ref.at[n], 0, short, row, 8) for n in range(6)]
        half_gap = csub((1.0 + 0.5 * h[0], 0.5 * h[1]), rho)
        wide = cmul(csqr(block), csqr(rho))
        low_w, high_w = cmul(low, wide), cmul(high, wide)
        whole = cscale(cinv(cmul(half_gap, cone(cmul(low, high_w)))), scale)
        turned = cmul(rho, whole)
        values = [
            cmul(cone(high_w), whole), cmul(cone(low), turned),
            cmul(cone(high), turned), cmul(cone(low_w), whole),
        ]
        pivot = (2.0 + h[0], h[1])
        inverse = cinv(pivot)
        values.append(inverse)
        for _ in range(count - 1):
            inverse = cinv(csub(pivot, inverse))
            values.append(inverse)
        near = far = None
        power = block
        for level in range(1, levels):
            taken = ((z >> (level - 1)) & 1) == 1
            if near is None:
                one = (jnp.ones_like(power[0]), jnp.zeros_like(power[0]))
                near, far = cpick(taken, power, one), cpick(taken, one, power)
            else:
                grown = cmul(cpick(taken, near, far), power)
                near, far = cpick(taken, grown, near), cpick(taken, far, grown)
            power = csqr(power)
            values.append(cpick(((z >> level) & 1) == 1, near, far))
        for n, value in enumerate(values):
            store(out_ref.at[n], 0, short, row, 8, value)

    each_strip(short, 8, strip)


def join_kernel(level, levels, flags_ref, sums_ref, came_ref, base_ref, out_ref):
    z = flags_ref[2]
    short = base_ref.shape[1] // 2
    rows = 2 * short
    above = ((z >> level) & 1) == 1
    last = level + 2 == levels
    upper = ((z >> (level + 1)) & 1) == 1

    def strip(row):
        block = load(base_ref.at[3], 0, short, row, 8)
        for _ in range(level):
            block = csqr(block)
        ahead, behind = load(sums_ref, 0, short, row, 8), load(sums_ref, rows, short, row, 8)
        ahead_c, behind_c = load(came_ref, 0, short, row, 8), load(came_ref, rows, short, row, 8)
        joined = cmore(cpick(above, ahead, ahead_c), block, cpick(above, ahead_c, ahead))
        joined_b = cmore(cpick(above, behind_c, behind), block, cpick(above, behind, behind_c))
        if last:
            store(out_ref, 0, short, row, 8, cpick(upper, joined_b, joined))
        else:
            store(out_ref, 0, short, row, 8, joined)
            store(out_ref, rows, short, row, 8, joined_b)

    each_strip(short, 8, strip)
    out_ref[pl.ds(out_ref.shape[0] - TAG, TAG), :] = (
        sums_ref[pl.ds(2 * rows, TAG), :] + came_ref[pl.ds(2 * rows, TAG), :]
    )


def solved(count, levels, z, scale, modes_ref, sums_ref, came_refs, base_ref, factors_ref, row):
    short = base_ref.shape[1] // 2
    rows = 2 * short

    def factor(n):
        return load(factors_ref.at[n], 0, short, row, 8)

    enter_f = enter_b = None
    for level in range(levels):
        above = ((z >> level) & 1) == 1
        base = 0 if level == levels - 1 else jnp.where(above, 0, rows)
        came = load(came_refs[level], base, short, row, 8)
        if level:
            came = cmul(factor(4 + count + level - 1), came)
        nought = (jnp.zeros_like(came[0]), jnp.zeros_like(came[0]))
        now_f, now_b = cpick(above, came, nought), cpick(above, nought, came)
        enter_f = now_f if enter_f is None else cadd(enter_f, now_f)
        enter_b = now_b if enter_b is None else cadd(enter_b, now_b)
    block = load(base_ref.at[3], 0, short, row, 8)
    all_f = cmore(load(sums_ref, 0, short, row, 8), block, enter_f)
    all_b = cmore(load(sums_ref, rows, short, row, 8), block, enter_b)
    below = cmore(cmul(factor(0), enter_f), factor(1), all_b)
    above = cmore(cmul(factor(3), enter_b), factor(2), all_f)
    planes = [cscale(load(modes_ref, l * rows, short, row, 8), scale) for l in range(count)]
    planes[0] = cadd(planes[0], below)
    planes[-1] = cadd(planes[-1], above)
    for l in range(1, count):
        planes[l] = cmore(planes[l], factor(4 + l - 1), planes[l - 1])
    planes[-1] = cmul(factor(4 + count - 1), planes[-1])
    for l in range(count - 2, -1, -1):
        planes[l] = cmul(factor(4 + l), cadd(planes[l], planes[l + 1]))
    return below, planes, above


def middle_kernel(
    chunk, count, levels, flags_ref, numbers_ref, wave_eig_ref, sine_ref, faces_ref, field_ref,
    modes_ref, base_ref, factors_ref, sums_ref, *refs,
):
    came_refs, (found_ref, next_ref, next_sums_ref) = refs[:levels], refs[levels : levels + 3]
    give_refs, work_ref = refs[levels + 3 : -1], refs[-1]
    q, h, z = flags_ref[0], flags_ref[1], flags_ref[2]
    scale, s_re, s_im = numbers_ref[2], numbers_ref[4], numbers_ref[5]
    short = base_ref.shape[1] // 2
    rows = 2 * short
    width = base_ref.shape[2]

    def solve(row):
        below, planes, above = solved(
            count, levels, z, scale, modes_ref, sums_ref, came_refs, base_ref, factors_ref, row
        )
        store(work_ref, 0, short, row, 8, below)
        store(work_ref, (count + 1) * rows, short, row, 8, above)
        for l in range(count):
            store(work_ref, (l + 1) * rows, short, row, 8, planes[l])
            store(found_ref, l * rows, short, row, 8, planes[l])

    each_strip(short, 8, solve)
    sine_rows(work_ref, work_ref, sine_ref, (count + 2) * rows)

    def residual(i, total):
        row = pl.multiple_of(i * 8, 8)
        eigen = wave_eig_ref[q, rows_at((h * CHUNKS + chunk) * short + row, 8), :]
        under = load(work_ref, 0, short, row, 8)
        here = load(work_ref, rows, short, row, 8)
        for l in range(count):
            over = load(work_ref, (l + 2) * rows, short, row, 8)
            diag, cell, right, left, low, high = [faces_ref[n, pl.ds(l, 1), :] for n in range(6)]
            diag = s_re + (diag + cell * eigen)
            value = []
            for c in range(2):
                v = diag * here[c] - right * pltpu.roll(here[c], width - 1, 1)
                v = v - left * pltpu.roll(here[c], 1, 1)
                value.append(v - (low * under[c] + high * over[c]))
            value = (value[0] - s_im * here[1], value[1] + s_im * here[0])
            value = csub(load(field_ref, l * rows, short, row, 8), value)
            total = total + squares_of(value)
            store(work_ref, l * rows, short, row, 8, value)
            under, here = here, over
        return total

    total = lax.fori_loop(0, short // 8, residual, jnp.zeros((8, width), jnp.float32), unroll=2)
    sine_rows(work_ref, next_ref, sine_ref, count * rows)

    def sums(row):
        rho, cross_f, cross_b = [load(base_ref.at[n], 0, short, row, 8) for n in range(3)]
        planes = [load(next_ref, l * rows, short, row, 8) for l in range(count)]
        ahead, behind = sums_of(planes, rho, cross_f, cross_b)
        store(next_sums_ref, 0, short, row, 8, ahead)
        store(next_sums_ref, rows, short, row, 8, behind)

    each_strip(short, 8, sums)
    next_sums_ref[pl.ds(2 * rows, TAG), :] = sums_ref[pl.ds(2 * rows, TAG), :]
    next_sums_ref[pl.ds(2 * rows + 1, 1), :] = jnp.sum(total, axis=0, keepdims=True)
    fill_give(z, rows, next_sums_ref, give_refs)


def end_kernel(
    count, levels, flags_ref, numbers_ref, sine_ref, found_ref, modes_ref, base_ref,
    factors_ref, sums_ref, *refs,
):
    came_refs, out_refs, work_ref = refs[:levels], refs[-1 - GROUP : -1], refs[-1]
    before_refs = refs[levels + (levels > 1) : -1 - GROUP]
    z, member = flags_ref[2], flags_ref[3]
    scale = numbers_ref[2]
    short = base_ref.shape[1] // 2
    rows = 2 * short

    def solve(row):
        _, planes, _ = solved(
            count, levels, z, scale, modes_ref, sums_ref, came_refs, base_ref, factors_ref, row
        )
        for l in range(count):
            before = load(found_ref, l * rows, short, row, 8)
            store(work_ref, l * rows, short, row, 8, cadd(before, planes[l]))

    each_strip(short, 8, solve)
    sine_rows(work_ref, work_ref, sine_ref, count * rows)
    part = count // GROUP * rows
    tag_refs = (refs[levels] if levels > 1 else sums_ref, came_refs[-1])
    tag = None
    for ref in tag_refs:
        part_tag = ref[pl.ds(ref.shape[0] - TAG, TAG), :]
        tag = part_tag if tag is None else tag + part_tag
    for d in range(GROUP):
        start, whole = 0, tag
        if d in JOINT:
            held = len(before_refs) // len(JOINT)
            for ref in before_refs[JOINT.index(d) * held : (JOINT.index(d) + 1) * held]:
                out_refs[d][pl.ds(start, part), :] = ref[pl.ds(0, part), :]
                start, whole = start + part, whole + tag_of(ref)
        out_refs[d][pl.ds(start, part), :] = work_ref[rows_at((member ^ d) * part, part), :]
        out_refs[d][pl.ds(start + part, TAG), :] = whole


smem = pl.BlockSpec(memory_space=pltpu.SMEM)
vmem = pl.BlockSpec(memory_space=pltpu.VMEM)
unread = pl.BlockSpec(memory_space=pl.ANY)


def call(kernel, scalars, arrays, outs, scratch=(), flops=0, after=()):
    out_shape = [jax.ShapeDtypeStruct(shape, jnp.float32) for shape in outs]
    head = len(scalars) + len(arrays)

    def run(*refs):
        kernel(*refs[:head], *refs[head + len(after) :])

    moved = sum(a.size * a.dtype.itemsize for a in arrays) + sum(4 * int(np.prod(s)) for s in outs)
    held = moved + sum(4 * int(np.prod(s)) for s in scratch)
    return pl.pallas_call(
        run,
        out_shape=out_shape,
        in_specs=[smem] * len(scalars) + [vmem] * len(arrays) + [unread] * len(after),
        out_specs=[smem if len(shape) == 1 else vmem for shape in outs],
        scratch_shapes=[pltpu.VMEM(shape, jnp.float32) for shape in scratch],
        compiler_params=pltpu.CompilerParams(vmem_limit_bytes=held + 4 * 2**20),
        cost_estimate=pl.CostEstimate(flops=flops, bytes_accessed=moved, transcendentals=0),
    )(*scalars, *arrays, *after)


def pair_up(array, groups, flip):
    return lax.ppermute(array, "gz", [(i, i ^ flip) for i in range(groups)])


def step_by(array, groups, distance):
    return lax.ppermute(
        array, "gz", [(i, i + distance) for i in range(groups) if 0 <= i + distance < groups]
    )


def body(source, layer_ids, conduct_table, shift):
    planes, length_x, length_y = source.shape[1:]
    groups = lax.axis_size("gz")
    blocks = groups // GROUP
    levels = blocks.bit_length() - 1
    count = GROUP * planes
    length_z = planes * groups
    full = length_x // RADIX
    short = full // (HALVES * CHUNKS)
    rows = 2 * short
    if blocks < 2 or groups != GROUP << levels or planes > 2 or short % 8 or length_x != RADIX * full:
        raise ValueError("unsupported layout")
    me = lax.axis_index("gz")
    member = me % GROUP
    flags = jnp.stack([member % RADIX, member // RADIX, me // GROUP, member]).astype(jnp.int32)

    wave = wave_tables(length_x)
    wave_f = jnp.asarray(np.concatenate(two_terms(wave), axis=1))
    wave_b = jnp.asarray(np.concatenate(two_terms(np.swapaxes(wave, 1, 2) / length_x), axis=1))
    sine = jnp.asarray(two_terms(sine_table(length_y)))
    wave_eig = np.broadcast_to(wave_eigen(length_x)[:, :, None], (RADIX, full, length_y))
    wave_eig = jnp.asarray(np.ascontiguousarray(wave_eig).astype(np.float32))
    sine_eig = jnp.asarray(np.tile(sine_eigen(length_y)[None, :], (8, 1)).astype(np.float32))

    chunks = range(CHUNKS)
    row_block = (TAG, length_y)
    block = (count * rows, length_y)
    sums_block = (2 * rows + TAG, length_y)
    single = (rows + TAG, length_y)
    part = (planes * rows + TAG, length_y)
    parts = (CHUNKS * planes * rows + TAG, length_y)
    gives = [single] if levels == 1 else []
    dots = 6 * length_y * length_y

    (cells,) = call(conduct_kernel, [conduct_table], [layer_ids], [row_block])
    if levels == 1:
        below = above = pair_up(cells, groups, GROUP)
        totals = [cells, below]
    else:
        below = step_by(cells, groups, GROUP)
        above = step_by(cells, groups, -GROUP)
        total = cells
        for level in range(levels):
            (total,) = call(add_kernel, [], [total, pair_up(total, groups, GROUP << level)], [row_block])
        totals = [total]

    parted = source.reshape(2, planes, RADIX, full, length_y)
    spectra = {}
    placed = [cells]
    tags = [cells, below, above, *totals]
    for d in (2, 0, 3, 1):
        early = d == 2
        made = call(
            functools.partial(forward_kernel, d, 0 if early else len(tags)), [flags],
            [parted, wave_f, *([] if early else tags)], [part] * (HALVES * CHUNKS),
            scratch=[(planes, 2 * full, length_y)], flops=planes * 2 * full * dots, after=placed,
        )
        if early:
            made = call(
                functools.partial(tagged_kernel, planes, len(made)), [], [*made, *tags], [part] * len(made),
            )
        placed = made[:1]
        for n in range(HALVES):
            for t in chunks:
                spectra[d + RADIX * n, t] = made[n * CHUNKS + t]
    for t in chunks:
        for d in (6, 2, 4, 7, 3, 5, 1):
            if t == 0 or d not in JOINT:
                spectra[d, t] = pair_up(spectra[d, t], groups, d)

    state = [{} for _ in chunks]

    def exchange(st, after):
        sums, give = st["sums"][0], st["sums"][-1]
        st["came"], st["tags"] = [], []
        for level in range(levels):
            st["came"].append(pair_up(give, groups, GROUP << level))
            if level + 1 < levels:
                shape = single if level + 2 == levels else sums_block
                (give,) = call(
                    functools.partial(join_kernel, level, levels), [flags], [sums, st["came"][-1], st["base"]],
                    [shape], after=after,
                )
                sums = give
                st["tags"] = [give[-TAG:]]

    def start(t, after):
        st = state[t]
        outs = [block, block, (6, rows, length_y), sums_block, *gives]
        made = call(
            functools.partial(start_kernel, t, planes, blocks, length_y * length_z),
            [flags, state[0]["numbers"] if t else shift],
            [wave_eig, sine_eig, sine] + [spectra[d, t] for d in range(GROUP)],
            outs if t else [*outs, (6,)], flops=count * rows * dots, after=after,
        )
        if not t:
            *made, st["numbers"] = made
        st["field"], st["modes"], st["base"], *st["sums"] = made
        exchange(st, [])
        return [st["sums"][-1]]

    def faces(t, after):
        state[t]["faces"] = call(
            functools.partial(faces_kernel, planes, blocks), [flags], [spectra[d, 0] for d in range(GROUP)],
            [(6, count, length_y)], scratch=[(count + 16, length_y), row_block, row_block], after=after,
        )[0]
        return [state[t]["faces"]]

    def factors(t, after):
        st = state[t]
        (st["factors"],) = call(
            functools.partial(factors_kernel, t, count, levels), [flags, state[0]["numbers"]],
            [wave_eig, sine_eig, st["base"]], [(4 + count + levels - 1, rows, length_y)], after=after,
        )
        return [st["factors"]]

    def middle(t, after):
        st = state[t]
        st["found"], st["modes"], *st["sums"] = call(
            functools.partial(middle_kernel, t, count, levels), [flags, state[0]["numbers"]],
            [wave_eig, sine, state[0]["faces"], st["field"], st["modes"], st["base"], st["factors"], st["sums"][0], *st["came"]],
            [block, block, sums_block, *gives], scratch=[((count + 2) * rows, length_y)],
            flops=(2 * count + 2) * rows * dots, after=after,
        )
        exchange(st, [])
        return [st["sums"][-1]]

    def end(t, after):
        st = state[t]
        last = t == CHUNKS - 1
        before = [state[u]["made"][d] for d in JOINT for u in range(t)] if last else []
        st["made"] = call(
            functools.partial(end_kernel, count, levels), [flags, state[0]["numbers"]],
            [sine, st["found"], st["modes"], st["base"], st["factors"], st["sums"][0], *st["came"], *st["tags"], *before],
            [parts if last and d in JOINT else part for d in range(GROUP)],
            scratch=[block], flops=count * rows * dots, after=after,
        )
        st["answers"] = {d: st["made"][d] for d in SENDS[t]}
        return [st["made"][0]]

    def held(array, after):
        return lax.optimization_barrier((array, *after))[0]

    def answer(t, distances):
        answers = state[t]["answers"]
        for d in distances:
            answers[d] = pair_up(answers[d], groups, d)

    placed = []
    for step in (start, faces, factors):
        placed = step(0, placed)
    for d in JOINT:
        spectra[d, 1] = pair_up(held(spectra[d, 1], placed), groups, d)
    for step, t in ((middle, 0), (start, 1), (factors, 1), (end, 0)):
        placed = step(t, placed)
    answer(0, SENDS[0][:-1])
    placed = middle(1, placed)
    end(1, [*placed, *[state[0]["answers"][d] for d in SENDS[0][:2]]])
    answer(1, SENDS[1][:-1])
    return call(
        functools.partial(backward_kernel, planes, length_x * length_x * length_y * length_z),
        [flags], [wave_b] + [state[t]["answers"][d] for t, d in ANSWERS],
        [(2, planes, length_x, length_y), (2,)],
        scratch=[(planes, RADIX, 2 * full, length_y), (RADIX, planes, 2 * full, length_y)],
        flops=planes * RADIX * 2 * full * dots,
    )


def solution(mesh):
    placed = (P(None, ("node", "gz"), None, None), P(("node", "gz"), None), P(), P("node"))
    return jax.shard_map(
        body,
        mesh=mesh,
        in_specs=placed,
        out_specs=(P(None, ("node", "gz"), None, None), P("node")),
        check_vma=False,
    )
```

profile of v0, /device:TPU:0, one launch (start us, length us, event | category | flops | bytes accessed | tf_op | source)
XLA Modules:
  0.0 89.7 jit_solution(3168564248414302949)
XLA Ops:
  0.6 0.7 copy-done.7
  1.3 0.7 copy-done.9
  2.0 0.6 shard_map.104.refs_3_.refs_4_.refs_7_.refs_6_
  2.5 4.1 %collective-permute-start = (f32[8,256]{1,0:T(8,128)S(1)}, f32[8,256]{1,0:T(8,128)S(1)}, u32[]{:S(2)}, u32[]{:S(2)}) collective-permute-start(f32[8,256]{1,0:T(8,128)S(1)} %shard_map.104.refs_3_.refs_4_.refs_7_.refs_6_), channel_id=1, source_target_pairs={{0,8},{1,9},{2,10},{3,11},{4,12},{5,13},{6,14},{7,15},{8,0},{9,1},... | collective-permute-start | bytes 24584 | tf_op jit(solution)/shard_map/ppermute | solution.py:635
  6.6 0.1 pad_add_fusion.refs_0_
  6.7 1.6 %copy-done = f32[2,2,512,256]{3,2,1,0:T(8,128)S(1)} copy-done((f32[2,2,512,256]{3,2,1,0:T(8,128)S(1)}, f32[2,2,512,256]{3,2,1,0:T(8,128)}, u32[]{:S(2)}) %copy-start) | copy-done | bytes 2097176
  8.3 1.2 %copy-done.3 = bf16[4,512,256]{2,1,0:T(8,128)(2,1)S(1)} copy-done((bf16[4,512,256]{2,1,0:T(8,128)(2,1)S(1)}, bf16[4,512,256]{2,1,0:T(8,128)(2,1)}, u32[]{:S(2)}) %copy-start.3) | copy-done | bytes 1048600
  9.5 1.1 %shard_map.105 = (f32[136,256]{1,0:T(8,128)S(1)}, f32[136,256]{1,0:T(8,128)S(1)}, f32[136,256]{1,0:T(8,128)S(1)}, f32[136,256]{1,0:T(8,128)S(1)}) custom-call(s32[4]{0:T(128)S(1)} %pad_add_fusion.refs_0_, f32[2,2,4,128,256]{4,3,2,1,0:T(8,128)S(1)} %bitcast.5, bf16[4,512,256]{2,1,0:T(8,128)(2,1)S(1)} %copy-done.3, ...), custom_call_target="tpu_custom_call" | custom-call | flops 201326592 | bytes 3702784 | tf_op jit(solution)/shard_map/pallas_call | solution.py:623
  10.7 0.0 collective-permute-done.refs_5_.refs_6_.refs_8_.refs_4_.refs_7_
  10.7 2.6 %collective-permute-start.6 = (f32[136,256]{1,0:T(8,128)S(1)}, f32[136,256]{1,0:T(8,128)S(1)}, u32[]{:S(2)}, u32[]{:S(2)}) collective-permute-start(f32[136,256]{1,0:T(8,128)S(1)} %get-tuple-element.69), channel_id=1, source_target_pairs={{0,6},{1,7},{2,4},{3,5},{4,2},{5,3},{6,0},{7,1},{8,14},{9,15},{10,... | collective-permute-start | bytes 417800 | tf_op jit(solution)/shard_map/ppermute | solution.py:635
  13.3 0.5 collective-permute-start.2
  13.8 1.1 %shard_map.107 = (f32[136,256]{1,0:T(8,128)S(1)}, f32[136,256]{1,0:T(8,128)S(1)}, f32[136,256]{1,0:T(8,128)S(1)}, f32[136,256]{1,0:T(8,128)S(1)}) custom-call(s32[4]{0:T(128)S(1)} %pad_add_fusion.refs_0_, f32[2,2,4,128,256]{4,3,2,1,0:T(8,128)S(1)} %bitcast.6, bf16[4,512,256]{2,1,0:T(8,128)(2,1)S(1)} %copy-done.3, ...), custom_call_target="tpu_custom_call" | custom-call | flops 201326592 | bytes 3743744 | tf_op jit(solution)/shard_map/pallas_call | solution.py:623
  15.0 0.5 collective-permute-start.4
  15.5 1.1 %shard_map.108 = (f32[136,256]{1,0:T(8,128)S(1)}, f32[136,256]{1,0:T(8,128)S(1)}, f32[136,256]{1,0:T(8,128)S(1)}, f32[136,256]{1,0:T(8,128)S(1)}) custom-call(s32[4]{0:T(128)S(1)} %pad_add_fusion.refs_0_, f32[2,2,4,128,256]{4,3,2,1,0:T(8,128)S(1)} %bitcast.7, bf16[4,512,256]{2,1,0:T(8,128)(2,1)S(1)} %copy-done.3, ...), custom_call_target="tpu_custom_call" | custom-call | flops 201326592 | bytes 3743744 | tf_op jit(solution)/shard_map/pallas_call | solution.py:623
  16.6 0.0 copy-start.2
  16.6 0.0 copy-start.4
  16.6 0.0 copy-start.6
  16.7 0.0 copy-start.8
  16.7 0.9 %collective-permute-start.7 = (f32[136,256]{1,0:T(8,128)S(1)}, f32[136,256]{1,0:T(8,128)S(1)}, u32[]{:S(2)}, u32[]{:S(2)}) collective-permute-start(f32[136,256]{1,0:T(8,128)S(1)} %get-tuple-element.70), channel_id=1, source_target_pairs={{0,7},{1,6},{2,5},{3,4},{4,3},{5,2},{6,1},{7,0},{8,15},{9,14},{10,... | collective-permute-start | bytes 417800 | tf_op jit(solution)/shard_map/ppermute | solution.py:635
  17.6 1.9 %collective-permute-start.3 = (f32[136,256]{1,0:T(8,128)S(1)}, f32[136,256]{1,0:T(8,128)S(1)}, u32[]{:S(2)}, u32[]{:S(2)}) collective-permute-start(f32[136,256]{1,0:T(8,128)S(1)} %get-tuple-element.65.refs_8_), channel_id=1, source_target_pairs={{0,3},{1,2},{2,1},{3,0},{4,7},{5,6},{6,5},{7,4},{8,11},{9,10},{10,... | collective-permute-start | bytes 417800 | tf_op jit(solution)/shard_map/ppermute | solution.py:635
  19.5 1.1 %shard_map.109 = (f32[136,256]{1,0:T(8,128)S(1)}, f32[136,256]{1,0:T(8,128)S(1)}, f32[136,256]{1,0:T(8,128)S(1)}, f32[136,256]{1,0:T(8,128)S(1)}) custom-call(s32[4]{0:T(128)S(1)} %pad_add_fusion.refs_0_, f32[2,2,4,128,256]{4,3,2,1,0:T(8,128)S(1)} %bitcast.8, bf16[4,512,256]{2,1,0:T(8,128)(2,1)S(1)} %copy-done.3, ...), custom_call_target="tpu_custom_call" | custom-call | flops 201326592 | bytes 3743744 | tf_op jit(solution)/shard_map/pallas_call | solution.py:623
  20.6 0.1 collective-permute-start.1
  20.7 0.0 collective-permute-done.2.refs_7_.refs_3_
  20.7 0.5 collective-permute-start.5
  21.3 1.5 %collective-permute-start.11 = (f32[136,256]{1,0:T(8,128)S(1)}, f32[136,256]{1,0:T(8,128)S(1)}, u32[]{:S(2)}, u32[]{:S(2)}) collective-permute-start(f32[136,256]{1,0:T(8,128)S(1)} %get-tuple-element.84), channel_id=1, source_target_pairs={{0,2},{1,3},{2,0},{3,1},{4,6},{5,7},{6,4},{7,5},{8,10},{9,11},{10,... | collective-permute-start | bytes 417800 | tf_op jit(solution)/shard_map/ppermute | solution.py:635
  22.8 0.9 %collective-permute-done.7.refs_12_.refs_8_ = f32[136,256]{1,0:T(8,128)S(1)} collective-permute-done((f32[136,256]{1,0:T(8,128)S(1)}, f32[136,256]{1,0:T(8,128)S(1)}, u32[]{:S(2)}, u32[]{:S(2)}) %collective-permute-start.7) | collective-permute-done | bytes 139296 | tf_op jit(solution)/shard_map/ppermute | solution.py:635
  23.7 1.8 %collective-permute-start.15 = (f32[136,256]{1,0:T(8,128)S(1)}, f32[136,256]{1,0:T(8,128)S(1)}, u32[]{:S(2)}, u32[]{:S(2)}) collective-permute-start(f32[136,256]{1,0:T(8,128)S(1)} %get-tuple-element.89), channel_id=1, source_target_pairs={{0,6},{1,7},{2,4},{3,5},{4,2},{5,3},{6,0},{7,1},{8,14},{9,15},{10,... | collective-permute-start | bytes 417800 | tf_op jit(solution)/shard_map/ppermute | solution.py:635
  25.5 0.7 collective-permute-done.3.refs_8_.refs_4_
  26.2 0.1 collective-permute-done.5.refs_10_.refs_6_
  26.2 2.5 %shard_map.110 = (f32[1024,256]{1,0:T(8,128)S(1)}, f32[1024,256]{1,0:T(8,128)S(1)}, f32[6,64,256]{2,1,0:T(8,128)S(1)}, f32[136,256]{1,0:T(8,128)S(1)}, f32[72,256]{1,0:T(8,128)S(1)}, /*index=5*/f32[6]{0:T(128)S(1)}) custom-call(s32[4]{0:T(128)S(1)} %pad_add_fusion.refs_0_, f32[2]{0:T(128)S(1)} %copy-done.8, f32[4,128,256]{2,1,0:T(8,128)S(1)} %copy-done.2, ...), custom_call_target="tpu_custom_call" | custom-call | flops 402653184 | bytes 4612120 | tf_op jit(solution)/shard_map/pallas_call | solution.py:623
  28.7 0.6 collective-permute-start.8
  29.3 1.0 %collective-permute-start.13 = (f32[136,256]{1,0:T(8,128)S(1)}, f32[136,256]{1,0:T(8,128)S(1)}, u32[]{:S(2)}, u32[]{:S(2)}) collective-permute-start(f32[136,256]{1,0:T(8,128)S(1)} %get-tuple-element.86), channel_id=1, source_target_pairs={{0,4},{1,5},{2,6},{3,7},{4,0},{5,1},{6,2},{7,3},{8,12},{9,13},{10,... | collective-permute-start | bytes 417800 | tf_op jit(solution)/shard_map/ppermute | solution.py:635
  30.3 1.1 %collective-permute-start.12 = (f32[136,256]{1,0:T(8,128)S(1)}, f32[136,256]{1,0:T(8,128)S(1)}, u32[]{:S(2)}, u32[]{:S(2)}) collective-permute-start(f32[136,256]{1,0:T(8,128)S(1)} %get-tuple-element.85), channel_id=1, source_target_pairs={{0,3},{1,2},{2,1},{3,0},{4,7},{5,6},{6,5},{7,4},{8,11},{9,10},{10,... | collective-permute-start | bytes 417800 | tf_op jit(solution)/shard_map/ppermute | solution.py:635
  31.4 0.7 shard_map.111.refs_5_.refs_4_
  32.0 0.9 shard_map.112.refs_8_.refs_11_.refs_6_
  33.0 1.2 %collective-permute-start.16 = (f32[136,256]{1,0:T(8,128)S(1)}, f32[136,256]{1,0:T(8,128)S(1)}, u32[]{:S(2)}, u32[]{:S(2)}) collective-permute-start(f32[136,256]{1,0:T(8,128)S(1)} %get-tuple-element.90), channel_id=1, source_target_pairs={{0,7},{1,6},{2,5},{3,4},{4,3},{5,2},{6,1},{7,0},{8,15},{9,14},{10,... | collective-permute-start | bytes 417800 | tf_op jit(solution)/shard_map/ppermute | solution.py:635
  34.2 0.7 collective-permute-start.10
  34.8 1.6 %collective-permute-done.8.refs_10_ = f32[72,256]{1,0:T(8,128)S(1)} collective-permute-done((f32[72,256]{1,0:T(8,128)S(1)}, f32[72,256]{1,0:T(8,128)S(1)}, u32[]{:S(2)}, u32[]{:S(2)}) %collective-permute-start.8) | collective-permute-done | bytes 73760 | tf_op jit(solution)/shard_map/ppermute | solution.py:635
  36.5 5.2 %shard_map.113 = (f32[1024,256]{1,0:T(8,128)S(1)}, f32[1024,256]{1,0:T(8,128)S(1)}, f32[136,256]{1,0:T(8,128)S(1)}, f32[72,256]{1,0:T(8,128)S(1)}) custom-call(s32[4]{0:T(128)S(1)} %pad_add_fusion.refs_0_, f32[6]{0:T(128)S(1)} %get-tuple-element.71.refs_1_, f32[4,128,256]{2,1,0:T(8,128)S(1)} %copy-done.2, bf16[2,256,256]{2,1,0:T(8,128)(2,1)S(1)} %copy-done.4, ...), custom_call_target="tpu_custom_call" | custom-call | flops 855638016 | bytes 7208960 | tf_op jit(solution)/shard_map/pallas_call | solution.py:623
  41.6 1.3 %collective-permute-start.9 = (f32[72,256]{1,0:T(8,128)S(1)}, f32[72,256]{1,0:T(8,128)S(1)}, u32[]{:S(2)}, u32[]{:S(2)}) collective-permute-start(f32[72,256]{1,0:T(8,128)S(1)} %get-tuple-element.80.refs_13_), channel_id=1, source_target_pairs={{0,8},{1,9},{2,10},{3,11},{4,12},{5,13},{6,14},{7,15},{8,0},{9,1},... | collective-permute-start | bytes 221192 | tf_op jit(solution)/shard_map/ppermute | solution.py:635
  42.9 0.4 collective-permute-done.14.refs_10_
  43.4 1.7 %shard_map.114 = (f32[1024,256]{1,0:T(8,128)S(1)}, f32[1024,256]{1,0:T(8,128)S(1)}, f32[6,64,256]{2,1,0:T(8,128)S(1)}, f32[136,256]{1,0:T(8,128)S(1)}, f32[72,256]{1,0:T(8,128)S(1)}) custom-call(s32[4]{0:T(128)S(1)} %pad_add_fusion.refs_0_, f32[6]{0:T(128)S(1)} %get-tuple-element.71.refs_1_, f32[4,128,256]{2,1,0:T(8,128)S(1)} %copy-done.2, ...), custom_call_target="tpu_custom_call" | custom-call | flops 402653184 | bytes 4612096 | tf_op jit(solution)/shard_map/pallas_call | solution.py:623
  45.1 1.4 %collective-permute-start.22 = (f32[72,256]{1,0:T(8,128)S(1)}, f32[72,256]{1,0:T(8,128)S(1)}, u32[]{:S(2)}, u32[]{:S(2)}) collective-permute-start(f32[72,256]{1,0:T(8,128)S(1)} %get-tuple-element.92.refs_5_), channel_id=1, source_target_pairs={{0,8},{1,9},{2,10},{3,11},{4,12},{5,13},{6,14},{7,15},{8,0},{9,1},... | collective-permute-start | bytes 221192 | tf_op jit(solution)/shard_map/ppermute | solution.py:635
  46.4 0.9 shard_map.115.refs_9_.refs_8_.refs_6_
  47.3 1.2 %collective-permute-done.9.refs_8_ = f32[72,256]{1,0:T(8,128)S(1)} collective-permute-done((f32[72,256]{1,0:T(8,128)S(1)}, f32[72,256]{1,0:T(8,128)S(1)}, u32[]{:S(2)}, u32[]{:S(2)}) %collective-permute-start.9) | collective-permute-done | bytes 73760 | tf_op jit(solution)/shard_map/ppermute | solution.py:635
  48.5 1.6 %shard_map.116 = (f32[136,256]{1,0:T(8,128)S(1)}, f32[136,256]{1,0:T(8,128)S(1)}, f32[136,256]{1,0:T(8,128)S(1)}, f32[136,256]{1,0:T(8,128)S(1)}, f32[136,256]{1...) custom-call(s32[4]{0:T(128)S(1)} %pad_add_fusion.refs_0_, ...), custom_call_target="tpu_custom_call" | custom-call | flops 402653184 | bytes 5390336 | tf_op jit(solution)/shard_map/pallas_call | solution.py:623
  50.2 1.3 %collective-permute-start.17 = (f32[136,256]{1,0:T(8,128)S(1)}, f32[136,256]{1,0:T(8,128)S(1)}, u32[]{:S(2)}, u32[]{:S(2)}) collective-permute-start(f32[136,256]{1,0:T(8,128)S(1)} %get-tuple-element.93), channel_id=1, source_target_pairs={{0,6},{1,7},{2,4},{3,5},{4,2},{5,3},{6,0},{7,1},{8,14},{9,15},{10,... | collective-permute-start | bytes 417800 | tf_op jit(solution)/shard_map/ppermute | solution.py:635
  51.4 0.8 collective-permute-start.19
  52.2 2.4 %collective-permute-start.20 = (f32[136,256]{1,0:T(8,128)S(1)}, f32[136,256]{1,0:T(8,128)S(1)}, u32[]{:S(2)}, u32[]{:S(2)}) collective-permute-start(f32[136,256]{1,0:T(8,128)S(1)} %get-tuple-element.96), channel_id=1, source_target_pairs={{0,3},{1,2},{2,1},{3,0},{4,7},{5,6},{6,5},{7,4},{8,11},{9,10},{10,... | collective-permute-start | bytes 417800 | tf_op jit(solution)/shard_map/ppermute | solution.py:635
  54.6 5.2 %shard_map.117 = (f32[1024,256]{1,0:T(8,128)S(1)}, f32[1024,256]{1,0:T(8,128)S(1)}, f32[136,256]{1,0:T(8,128)S(1)}, f32[72,256]{1,0:T(8,128)S(1)}) custom-call(s32[4]{0:T(128)S(1)} %pad_add_fusion.refs_0_, f32[6]{0:T(128)S(1)} %get-tuple-element.71.refs_1_, f32[4,128,256]{2,1,0:T(8,128)S(1)} %copy-done.2, bf16[2,256,256]{2,1,0:T(8,128)(2,1)S(1)} %copy-done.4, ...), custom_call_target="tpu_custom_call" | custom-call | flops 855638016 | bytes 7208960 | tf_op jit(solution)/shard_map/pallas_call | solution.py:623
  59.8 0.5 collective-permute-start.23
  60.3 5.9 %collective-permute-done.23.refs_8_ = f32[72,256]{1,0:T(8,128)S(1)} collective-permute-done((f32[72,256]{1,0:T(8,128)S(1)}, f32[72,256]{1,0:T(8,128)S(1)}, u32[]{:S(2)}, u32[]{:S(2)}) %collective-permute-start.23) | collective-permute-done | bytes 73760 | tf_op jit(solution)/shard_map/ppermute | solution.py:635
  66.2 0.0 copy-start.5
  66.2 1.6 %shard_map.118 = (f32[136,256]{1,0:T(8,128)S(1)}, f32[264,256]{1,0:T(8,128)S(1)}, f32[136,256]{1,0:T(8,128)S(1)}, f32[136,256]{1,0:T(8,128)S(1)}, f32[136,256]{1...) custom-call(s32[4]{0:T(128)S(1)} %pad_add_fusion.refs_0_, ...), custom_call_target="tpu_custom_call" | custom-call | flops 402653184 | bytes 5931008 | tf_op jit(solution)/shard_map/pallas_call | solution.py:623
  67.8 1.0 %collective-permute-start.24 = (f32[136,256]{1,0:T(8,128)S(1)}, f32[136,256]{1,0:T(8,128)S(1)}, u32[]{:S(2)}, u32[]{:S(2)}) collective-permute-start(f32[136,256]{1,0:T(8,128)S(1)} %get-tuple-element.108), channel_id=1, source_target_pairs={{0,2},{1,3},{2,0},{3,1},{4,6},{5,7},{6,4},{7,5},{8,10},{9,11},{10,... | collective-permute-start | bytes 417800 | tf_op jit(solution)/shard_map/ppermute | solution.py:635
  68.8 2.6 %collective-permute-start.25 = (f32[136,256]{1,0:T(8,128)S(1)}, f32[136,256]{1,0:T(8,128)S(1)}, u32[]{:S(2)}, u32[]{:S(2)}) collective-permute-start(f32[136,256]{1,0:T(8,128)S(1)} %get-tuple-element.109), channel_id=1, source_target_pairs={{0,6},{1,7},{2,4},{3,5},{4,2},{5,3},{6,0},{7,1},{8,14},{9,15},{10,... | collective-permute-start | bytes 417800 | tf_op jit(solution)/shard_map/ppermute | solution.py:635
  71.4 0.1 collective-permute-start.30
  71.5 2.0 %collective-permute-start.26 = (f32[136,256]{1,0:T(8,128)S(1)}, f32[136,256]{1,0:T(8,128)S(1)}, u32[]{:S(2)}, u32[]{:S(2)}) collective-permute-start(f32[136,256]{1,0:T(8,128)S(1)} %get-tuple-element.110), channel_id=1, source_target_pairs={{0,7},{1,6},{2,5},{3,4},{4,3},{5,2},{6,1},{7,0},{8,15},{9,14},{10,... | collective-permute-start | bytes 417800 | tf_op jit(solution)/shard_map/ppermute | solution.py:635
  73.6 2.5 %collective-permute-done.24.refs_8_ = f32[136,256]{1,0:T(8,128)S(1)} collective-permute-done((f32[136,256]{1,0:T(8,128)S(1)}, f32[136,256]{1,0:T(8,128)S(1)}, u32[]{:S(2)}, u32[]{:S(2)}) %collective-permute-start.24) | collective-permute-done | bytes 139296 | tf_op jit(solution)/shard_map/ppermute | solution.py:635
  76.1 2.1 %collective-permute-start.28 = (f32[136,256]{1,0:T(8,128)S(1)}, f32[136,256]{1,0:T(8,128)S(1)}, u32[]{:S(2)}, u32[]{:S(2)}) collective-permute-start(f32[136,256]{1,0:T(8,128)S(1)} %get-tuple-element.112), channel_id=1, source_target_pairs={{0,4},{1,5},{2,6},{3,7},{4,0},{5,1},{6,2},{7,3},{8,12},{9,13},{10,... | collective-permute-start | bytes 417800 | tf_op jit(solution)/shard_map/ppermute | solution.py:635
  78.2 5.7 %collective-permute-done.26.refs_10_ = f32[136,256]{1,0:T(8,128)S(1)} collective-permute-done((f32[136,256]{1,0:T(8,128)S(1)}, f32[136,256]{1,0:T(8,128)S(1)}, u32[]{:S(2)}, u32[]{:S(2)}) %collective-permute-start.26) | collective-permute-done | bytes 139296 | tf_op jit(solution)/shard_map/ppermute | solution.py:635
  83.9 0.5 collective-permute-done.27.refs_11_
  84.4 1.8 %collective-permute-done.28.refs_12_ = f32[136,256]{1,0:T(8,128)S(1)} collective-permute-done((f32[136,256]{1,0:T(8,128)S(1)}, f32[136,256]{1,0:T(8,128)S(1)}, u32[]{:S(2)}, u32[]{:S(2)}) %collective-permute-start.28) | collective-permute-done | bytes 139296 | tf_op jit(solution)/shard_map/ppermute | solution.py:635
  86.2 3.3 %shard_map.119 = (f32[2,2,512,256]{3,2,1,0:T(8,128)}, f32[2]{0:T(128)}) custom-call(s32[4]{0:T(128)S(1)} %pad_add_fusion.refs_0_, bf16[4,512,256]{2,1,0:T(8,128)(2,1)S(1)} %copy-done.5, f32[136,256]{1,0:T(8,128)S(1)} %collective-permute-done.17.refs_12_.refs_2_, f32[136,256]{1,0:T(8,128)S(1)} %collective-permute-done.18.refs_13_.refs_3_, ...), custom_call_target="tpu_custom_call" | custom-call | flops 805306368 | bytes 5357576 | tf_op jit(solution)/shard_map/pallas_call | solution.py:623
  (35 shorter events, 0.1 us)
Async XLA Ops:
  0.6 0.7 copy-start.7
  1.3 0.7 copy-start.9
  2.5 8.1 %collective-permute-start = (f32[8,256]{1,0:T(8,128)S(1)}, f32[8,256]{1,0:T(8,128)S(1)}, u32[]{:S(2)}, u32[]{:S(2)}) collective-permute-start(f32[8,256]{1,0:T(8,128)S(1)} %shard_map.104.refs_3_.refs_4_.refs_7_.refs_6_), channel_id=1, source_target_pairs={{0,8},{1,9},{2,10},{3,11},{4,12},{5,13},{6,14},{7,15},{8,0},{9,1},... | collective-permute-start | bytes 24584 | tf_op jit(solution)/shard_map/ppermute | solution.py:635
  6.7 1.6 %copy-start = (f32[2,2,512,256]{3,2,1,0:T(8,128)S(1)}, f32[2,2,512,256]{3,2,1,0:T(8,128)}, u32[]{:S(2)}) copy-start(f32[2,2,512,256]{3,2,1,0:T(8,128)} %param.9) | copy-start | bytes 6291460
  8.3 1.2 %copy-start.3 = (bf16[4,512,256]{2,1,0:T(8,128)(2,1)S(1)}, bf16[4,512,256]{2,1,0:T(8,128)(2,1)}, u32[]{:S(2)}) copy-start(bf16[4,512,256]{2,1,0:T(8,128)(2,1)} %constant.58.clone.refs_2_) | copy-start | bytes 3145732
  9.5 4.3 %copy-start.1 = (f32[2,2,512,256]{3,2,1,0:T(8,128)S(1)}, f32[2,2,512,256]{3,2,1,0:T(8,128)}, u32[]{:S(2)}) copy-start(f32[2,2,512,256]{3,2,1,0:T(8,128)} %param.9) | copy-start | bytes 6291460
  10.7 9.9 %collective-permute-start.6 = (f32[136,256]{1,0:T(8,128)S(1)}, f32[136,256]{1,0:T(8,128)S(1)}, u32[]{:S(2)}, u32[]{:S(2)}) collective-permute-start(f32[136,256]{1,0:T(8,128)S(1)} %get-tuple-element.69), channel_id=1, source_target_pairs={{0,6},{1,7},{2,4},{3,5},{4,2},{5,3},{6,0},{7,1},{8,14},{9,15},{10,... | collective-permute-start | bytes 417800 | tf_op jit(solution)/shard_map/ppermute | solution.py:635
  13.3 7.4 %collective-permute-start.2 = (f32[136,256]{1,0:T(8,128)S(1)}, f32[136,256]{1,0:T(8,128)S(1)}, u32[]{:S(2)}, u32[]{:S(2)}) collective-permute-start(f32[136,256]{1,0:T(8,128)S(1)} %get-tuple-element.63.refs_8_), channel_id=1, source_target_pairs={{0,2},{1,3},{2,0},{3,1},{4,6},{5,7},{6,4},{7,5},{8,10},{9,11},{10,... | collective-permute-start | bytes 417800 | tf_op jit(solution)/shard_map/ppermute | solution.py:635
  15.0 6.3 %collective-permute-start.4 = (f32[136,256]{1,0:T(8,128)S(1)}, f32[136,256]{1,0:T(8,128)S(1)}, u32[]{:S(2)}, u32[]{:S(2)}) collective-permute-start(f32[136,256]{1,0:T(8,128)S(1)} %get-tuple-element.67), channel_id=1, source_target_pairs={{0,4},{1,5},{2,6},{3,7},{4,0},{5,1},{6,2},{7,3},{8,12},{9,13},{10,... | collective-permute-start | bytes 417800 | tf_op jit(solution)/shard_map/ppermute | solution.py:635
  16.6 9.6 %copy-start.2 = (f32[4,128,256]{2,1,0:T(8,128)S(1)}, f32[4,128,256]{2,1,0:T(8,128)}, u32[]{:S(2)}) copy-start(f32[4,128,256]{2,1,0:T(8,128)} %constant.61.clone.refs_2_) | copy-start | bytes 1572868
  16.6 9.6 %copy-start.4 = (bf16[2,256,256]{2,1,0:T(8,128)(2,1)S(1)}, bf16[2,256,256]{2,1,0:T(8,128)(2,1)}, u32[]{:S(2)}) copy-start(bf16[2,256,256]{2,1,0:T(8,128)(2,1)} %constant.60.clone.refs_4_.refs_3_.refs_2_) | copy-start | bytes 786436
  16.6 9.6 %copy-start.6 = (f32[8,256]{1,0:T(8,128)S(1)}, f32[8,256]{1,0:T(8,128)}, u32[]{:S(2)}) copy-start(f32[8,256]{1,0:T(8,128)} %constant.62.clone.refs_3_) | copy-start | bytes 24580
  16.7 9.6 %copy-start.8 = (f32[2]{0:T(128)S(1)}, f32[2]{0:T(128)}, u32[]{:S(2)}) copy-start(f32[2]{0:T(128)} %refs_1_.4) | copy-start | bytes 28
  16.7 7.0 %collective-permute-start.7 = (f32[136,256]{1,0:T(8,128)S(1)}, f32[136,256]{1,0:T(8,128)S(1)}, u32[]{:S(2)}, u32[]{:S(2)}) collective-permute-start(f32[136,256]{1,0:T(8,128)S(1)} %get-tuple-element.70), channel_id=1, source_target_pairs={{0,7},{1,6},{2,5},{3,4},{4,3},{5,2},{6,1},{7,0},{8,15},{9,14},{10,... | collective-permute-start | bytes 417800 | tf_op jit(solution)/shard_map/ppermute | solution.py:635
  17.6 8.6 %collective-permute-start.3 = (f32[136,256]{1,0:T(8,128)S(1)}, f32[136,256]{1,0:T(8,128)S(1)}, u32[]{:S(2)}, u32[]{:S(2)}) collective-permute-start(f32[136,256]{1,0:T(8,128)S(1)} %get-tuple-element.65.refs_8_), channel_id=1, source_target_pairs={{0,3},{1,2},{2,1},{3,0},{4,7},{5,6},{6,5},{7,4},{8,11},{9,10},{10,... | collective-permute-start | bytes 417800 | tf_op jit(solution)/shard_map/ppermute | solution.py:635
  20.6 5.5 %collective-permute-start.1 = (f32[136,256]{1,0:T(8,128)S(1)}, f32[136,256]{1,0:T(8,128)S(1)}, u32[]{:S(2)}, u32[]{:S(2)}) collective-permute-start(f32[136,256]{1,0:T(8,128)S(1)} %get-tuple-element.66), channel_id=1, source_target_pairs={{0,1},{1,0},{2,3},{3,2},{4,5},{5,4},{6,7},{7,6},{8,9},{9,8},{10,11... | collective-permute-start | bytes 417800 | tf_op jit(solution)/shard_map/ppermute | solution.py:635
  20.7 5.5 %collective-permute-start.5 = (f32[136,256]{1,0:T(8,128)S(1)}, f32[136,256]{1,0:T(8,128)S(1)}, u32[]{:S(2)}, u32[]{:S(2)}) collective-permute-start(f32[136,256]{1,0:T(8,128)S(1)} %get-tuple-element.68), channel_id=1, source_target_pairs={{0,5},{1,4},{2,7},{3,6},{4,1},{5,0},{6,3},{7,2},{8,13},{9,12},{10,... | collective-permute-start | bytes 417800 | tf_op jit(solution)/shard_map/ppermute | solution.py:635
  21.3 11.7 %collective-permute-start.11 = (f32[136,256]{1,0:T(8,128)S(1)}, f32[136,256]{1,0:T(8,128)S(1)}, u32[]{:S(2)}, u32[]{:S(2)}) collective-permute-start(f32[136,256]{1,0:T(8,128)S(1)} %get-tuple-element.84), channel_id=1, source_target_pairs={{0,2},{1,3},{2,0},{3,1},{4,6},{5,7},{6,4},{7,5},{8,10},{9,11},{10,... | collective-permute-start | bytes 417800 | tf_op jit(solution)/shard_map/ppermute | solution.py:635
  23.7 10.4 %collective-permute-start.15 = (f32[136,256]{1,0:T(8,128)S(1)}, f32[136,256]{1,0:T(8,128)S(1)}, u32[]{:S(2)}, u32[]{:S(2)}) collective-permute-start(f32[136,256]{1,0:T(8,128)S(1)} %get-tuple-element.89), channel_id=1, source_target_pairs={{0,6},{1,7},{2,4},{3,5},{4,2},{5,3},{6,0},{7,1},{8,14},{9,15},{10,... | collective-permute-start | bytes 417800 | tf_op jit(solution)/shard_map/ppermute | solution.py:635
  28.7 7.7 %collective-permute-start.8 = (f32[72,256]{1,0:T(8,128)S(1)}, f32[72,256]{1,0:T(8,128)S(1)}, u32[]{:S(2)}, u32[]{:S(2)}) collective-permute-start(f32[72,256]{1,0:T(8,128)S(1)} %get-tuple-element.72.refs_9_), channel_id=1, source_target_pairs={{0,8},{1,9},{2,10},{3,11},{4,12},{5,13},{6,14},{7,15},{8,0},{9,1},... | collective-permute-start | bytes 221192 | tf_op jit(solution)/shard_map/ppermute | solution.py:635
  29.3 12.3 %collective-permute-start.13 = (f32[136,256]{1,0:T(8,128)S(1)}, f32[136,256]{1,0:T(8,128)S(1)}, u32[]{:S(2)}, u32[]{:S(2)}) collective-permute-start(f32[136,256]{1,0:T(8,128)S(1)} %get-tuple-element.86), channel_id=1, source_target_pairs={{0,4},{1,5},{2,6},{3,7},{4,0},{5,1},{6,2},{7,3},{8,12},{9,13},{10,... | collective-permute-start | bytes 417800 | tf_op jit(solution)/shard_map/ppermute | solution.py:635
  30.3 12.6 %collective-permute-start.12 = (f32[136,256]{1,0:T(8,128)S(1)}, f32[136,256]{1,0:T(8,128)S(1)}, u32[]{:S(2)}, u32[]{:S(2)}) collective-permute-start(f32[136,256]{1,0:T(8,128)S(1)} %get-tuple-element.85), channel_id=1, source_target_pairs={{0,3},{1,2},{2,1},{3,0},{4,7},{5,6},{6,5},{7,4},{8,11},{9,10},{10,... | collective-permute-start | bytes 417800 | tf_op jit(solution)/shard_map/ppermute | solution.py:635
  33.0 10.0 %collective-permute-start.16 = (f32[136,256]{1,0:T(8,128)S(1)}, f32[136,256]{1,0:T(8,128)S(1)}, u32[]{:S(2)}, u32[]{:S(2)}) collective-permute-start(f32[136,256]{1,0:T(8,128)S(1)} %get-tuple-element.90), channel_id=1, source_target_pairs={{0,7},{1,6},{2,5},{3,4},{4,3},{5,2},{6,1},{7,0},{8,15},{9,14},{10,... | collective-permute-start | bytes 417800 | tf_op jit(solution)/shard_map/ppermute | solution.py:635
  34.2 8.8 %collective-permute-start.10 = (f32[136,256]{1,0:T(8,128)S(1)}, f32[136,256]{1,0:T(8,128)S(1)}, u32[]{:S(2)}, u32[]{:S(2)}) collective-permute-start(f32[136,256]{1,0:T(8,128)S(1)} %get-tuple-element.83), channel_id=1, source_target_pairs={{0,1},{1,0},{2,3},{3,2},{4,5},{5,4},{6,7},{7,6},{8,9},{9,8},{10,11... | collective-permute-start | bytes 417800 | tf_op jit(solution)/shard_map/ppermute | solution.py:635
  36.5 6.9 %collective-permute-start.14 = (f32[136,256]{1,0:T(8,128)S(1)}, f32[136,256]{1,0:T(8,128)S(1)}, u32[]{:S(2)}, u32[]{:S(2)}) collective-permute-start(f32[136,256]{1,0:T(8,128)S(1)} %get-tuple-element.88), channel_id=1, source_target_pairs={{0,5},{1,4},{2,7},{3,6},{4,1},{5,0},{6,3},{7,2},{8,13},{9,12},{10,... | collective-permute-start | bytes 417800 | tf_op jit(solution)/shard_map/ppermute | solution.py:635
  41.6 6.9 %collective-permute-start.9 = (f32[72,256]{1,0:T(8,128)S(1)}, f32[72,256]{1,0:T(8,128)S(1)}, u32[]{:S(2)}, u32[]{:S(2)}) collective-permute-start(f32[72,256]{1,0:T(8,128)S(1)} %get-tuple-element.80.refs_13_), channel_id=1, source_target_pairs={{0,8},{1,9},{2,10},{3,11},{4,12},{5,13},{6,14},{7,15},{8,0},{9,1},... | collective-permute-start | bytes 221192 | tf_op jit(solution)/shard_map/ppermute | solution.py:635
  45.1 9.6 %collective-permute-start.22 = (f32[72,256]{1,0:T(8,128)S(1)}, f32[72,256]{1,0:T(8,128)S(1)}, u32[]{:S(2)}, u32[]{:S(2)}) collective-permute-start(f32[72,256]{1,0:T(8,128)S(1)} %get-tuple-element.92.refs_5_), channel_id=1, source_target_pairs={{0,8},{1,9},{2,10},{3,11},{4,12},{5,13},{6,14},{7,15},{8,0},{9,1},... | collective-permute-start | bytes 221192 | tf_op jit(solution)/shard_map/ppermute | solution.py:635
  50.2 16.0 %collective-permute-start.17 = (f32[136,256]{1,0:T(8,128)S(1)}, f32[136,256]{1,0:T(8,128)S(1)}, u32[]{:S(2)}, u32[]{:S(2)}) collective-permute-start(f32[136,256]{1,0:T(8,128)S(1)} %get-tuple-element.93), channel_id=1, source_target_pairs={{0,6},{1,7},{2,4},{3,5},{4,2},{5,3},{6,0},{7,1},{8,14},{9,15},{10,... | collective-permute-start | bytes 417800 | tf_op jit(solution)/shard_map/ppermute | solution.py:635
  51.4 14.8 %collective-permute-start.18 = (f32[136,256]{1,0:T(8,128)S(1)}, f32[136,256]{1,0:T(8,128)S(1)}, u32[]{:S(2)}, u32[]{:S(2)}) collective-permute-start(f32[136,256]{1,0:T(8,128)S(1)} %get-tuple-element.94), channel_id=1, source_target_pairs={{0,7},{1,6},{2,5},{3,4},{4,3},{5,2},{6,1},{7,0},{8,15},{9,14},{10,... | collective-permute-start | bytes 417800 | tf_op jit(solution)/shard_map/ppermute | solution.py:635
  51.4 20.0 %collective-permute-start.19 = (f32[136,256]{1,0:T(8,128)S(1)}, f32[136,256]{1,0:T(8,128)S(1)}, u32[]{:S(2)}, u32[]{:S(2)}) collective-permute-start(f32[136,256]{1,0:T(8,128)S(1)} %get-tuple-element.95), channel_id=1, source_target_pairs={{0,2},{1,3},{2,0},{3,1},{4,6},{5,7},{6,4},{7,5},{8,10},{9,11},{10,... | collective-permute-start | bytes 417800 | tf_op jit(solution)/shard_map/ppermute | solution.py:635
  52.2 19.2 %collective-permute-start.20 = (f32[136,256]{1,0:T(8,128)S(1)}, f32[136,256]{1,0:T(8,128)S(1)}, u32[]{:S(2)}, u32[]{:S(2)}) collective-permute-start(f32[136,256]{1,0:T(8,128)S(1)} %get-tuple-element.96), channel_id=1, source_target_pairs={{0,3},{1,2},{2,1},{3,0},{4,7},{5,6},{6,5},{7,4},{8,11},{9,10},{10,... | collective-permute-start | bytes 417800 | tf_op jit(solution)/shard_map/ppermute | solution.py:635
  59.8 6.4 %collective-permute-start.23 = (f32[72,256]{1,0:T(8,128)S(1)}, f32[72,256]{1,0:T(8,128)S(1)}, u32[]{:S(2)}, u32[]{:S(2)}) collective-permute-start(f32[72,256]{1,0:T(8,128)S(1)} %get-tuple-element.105.refs_11_), channel_id=1, source_target_pairs={{0,8},{1,9},{2,10},{3,11},{4,12},{5,13},{6,14},{7,15},{8,0},{9,1},... | collective-permute-start | bytes 221192 | tf_op jit(solution)/shard_map/ppermute | solution.py:635
  66.2 5.4 %collective-permute-start.21 = (f32[136,256]{1,0:T(8,128)S(1)}, f32[136,256]{1,0:T(8,128)S(1)}, u32[]{:S(2)}, u32[]{:S(2)}) collective-permute-start(f32[136,256]{1,0:T(8,128)S(1)} %get-tuple-element.97), channel_id=1, source_target_pairs={{0,4},{1,5},{2,6},{3,7},{4,0},{5,1},{6,2},{7,3},{8,12},{9,13},{10,... | collective-permute-start | bytes 417800 | tf_op jit(solution)/shard_map/ppermute | solution.py:635
  66.2 20.0 %copy-start.5 = (bf16[4,512,256]{2,1,0:T(8,128)(2,1)S(1)}, bf16[4,512,256]{2,1,0:T(8,128)(2,1)}, u32[]{:S(2)}) copy-start(bf16[4,512,256]{2,1,0:T(8,128)(2,1)} %constant.59.clone.refs_1_) | copy-start | bytes 3145732
  67.8 8.3 %collective-permute-start.24 = (f32[136,256]{1,0:T(8,128)S(1)}, f32[136,256]{1,0:T(8,128)S(1)}, u32[]{:S(2)}, u32[]{:S(2)}) collective-permute-start(f32[136,256]{1,0:T(8,128)S(1)} %get-tuple-element.108), channel_id=1, source_target_pairs={{0,2},{1,3},{2,0},{3,1},{4,6},{5,7},{6,4},{7,5},{8,10},{9,11},{10,... | collective-permute-start | bytes 417800 | tf_op jit(solution)/shard_map/ppermute | solution.py:635
  68.8 7.3 %collective-permute-start.25 = (f32[136,256]{1,0:T(8,128)S(1)}, f32[136,256]{1,0:T(8,128)S(1)}, u32[]{:S(2)}, u32[]{:S(2)}) collective-permute-start(f32[136,256]{1,0:T(8,128)S(1)} %get-tuple-element.109), channel_id=1, source_target_pairs={{0,6},{1,7},{2,4},{3,5},{4,2},{5,3},{6,0},{7,1},{8,14},{9,15},{10,... | collective-permute-start | bytes 417800 | tf_op jit(solution)/shard_map/ppermute | solution.py:635
  71.4 14.8 %collective-permute-start.29 = (f32[264,256]{1,0:T(8,128)S(1)}, f32[264,256]{1,0:T(8,128)S(1)}, u32[]{:S(2)}, u32[]{:S(2)}) collective-permute-start(f32[264,256]{1,0:T(8,128)S(1)} %get-tuple-element.113), channel_id=1, source_target_pairs={{0,5},{1,4},{2,7},{3,6},{4,1},{5,0},{6,3},{7,2},{8,13},{9,12},{10,... | collective-permute-start | bytes 811016 | tf_op jit(solution)/shard_map/ppermute | solution.py:635
  71.4 14.8 %collective-permute-start.30 = (f32[264,256]{1,0:T(8,128)S(1)}, f32[264,256]{1,0:T(8,128)S(1)}, u32[]{:S(2)}, u32[]{:S(2)}) collective-permute-start(f32[264,256]{1,0:T(8,128)S(1)} %get-tuple-element.114), channel_id=1, source_target_pairs={{0,1},{1,0},{2,3},{3,2},{4,5},{5,4},{6,7},{7,6},{8,9},{9,8},{10,11... | collective-permute-start | bytes 811016 | tf_op jit(solution)/shard_map/ppermute | solution.py:635
  71.5 12.4 %collective-permute-start.26 = (f32[136,256]{1,0:T(8,128)S(1)}, f32[136,256]{1,0:T(8,128)S(1)}, u32[]{:S(2)}, u32[]{:S(2)}) collective-permute-start(f32[136,256]{1,0:T(8,128)S(1)} %get-tuple-element.110), channel_id=1, source_target_pairs={{0,7},{1,6},{2,5},{3,4},{4,3},{5,2},{6,1},{7,0},{8,15},{9,14},{10,... | collective-permute-start | bytes 417800 | tf_op jit(solution)/shard_map/ppermute | solution.py:635
  76.1 8.3 %collective-permute-start.27 = (f32[136,256]{1,0:T(8,128)S(1)}, f32[136,256]{1,0:T(8,128)S(1)}, u32[]{:S(2)}, u32[]{:S(2)}) collective-permute-start(f32[136,256]{1,0:T(8,128)S(1)} %get-tuple-element.111), channel_id=1, source_target_pairs={{0,3},{1,2},{2,1},{3,0},{4,7},{5,6},{6,5},{7,4},{8,11},{9,10},{10,... | collective-permute-start | bytes 417800 | tf_op jit(solution)/shard_map/ppermute | solution.py:635
  76.1 10.1 %collective-permute-start.28 = (f32[136,256]{1,0:T(8,128)S(1)}, f32[136,256]{1,0:T(8,128)S(1)}, u32[]{:S(2)}, u32[]{:S(2)}) collective-permute-start(f32[136,256]{1,0:T(8,128)S(1)} %get-tuple-element.112), channel_id=1, source_target_pairs={{0,4},{1,5},{2,6},{3,7},{4,0},{5,1},{6,2},{7,3},{8,12},{9,13},{10,... | collective-permute-start | bytes 417800 | tf_op jit(solution)/shard_map/ppermute | solution.py:635
where the time goes:
time: 89.9 us; the launch traced here: 89.7 us
  starting transfers between devices  34.4 us (38%)
  Pallas kernels  28.6 us (32%)
  waiting for transfers between devices  21.4 us (24%)
  local copies, waits for them, and re-layouts  4.18 us (5%)
  between operations  1.02 us (1%)
    ppermute x31, starting transfers between devices, pair_up(): return lax.ppermute(array, 'gz', [(i, i ^ flip) for i in range(groups)])  34.4 us
    pallas_call x16, Pallas kernels, call(): pl.pallas_call(run, out_shape=out_shape, in_specs=[smem] * len(scalars) +...  28.6 us
    ppermute x31, waiting for transfers between devices, pair_up(): return lax.ppermute(array, 'gz', [(i, i ^ flip) for i in range(groups)])  21.4 us
    unnamed x20, local copies, waits for them, and re-layouts  4.18 us
  transfers between devices with their start and end apart: 31, of which 11 were waited for; matrix products, arithmetic and copies ran while one was open for 0% of the time, Pallas kernels for 28%

commit v1 on v0

--- a/solution.py
+++ b/solution.py
@@ -13,7 +13,7 @@
 HALVES = 2
 GROUP = RADIX * HALVES
 CHUNKS = 2
-SENDS = ((6, 7, 2, 3, 4, 0), (2, 6, 7, 3, 4, 5, 1, 0))
+SENDS = ((6, 7, 2, 3, 4, 0), (6, 2, 7, 3, 4, 5, 1, 0))
 ANSWERS = tuple((t, d) for t in range(CHUNKS) for d in SENDS[t])
 JOINT = (5, 1)
 TAG = 8

time: 89.9 us -> 89.8 us (level)
  waiting for transfers between devices: 21.4 us -> 23.8 us
  starting transfers between devices: 34.4 us -> 32 us
    ppermute x31, starting transfers between devices: 34.4 us -> 32 us  [pair_up(): return lax.ppermute(array, 'gz', [(i, i ^ flip) for i in range(groups)])]
    ppermute x31, waiting for transfers between devices: 21.4 us -> 23.8 us  [pair_up(): return lax.ppermute(array, 'gz', [(i, i ^ flip) for i in range(groups)])]
  transfers between devices with their start and end apart: 31 -> 31, of which waited for: 11 -> 12; matrix products, arithmetic and copies ran while one was open for 0% -> 0% of each run, Pallas kernels for 28% -> 28%
where the time goes in v1:
time: 89.8 us; the launch traced here: 89.6 us
  starting transfers between devices  32 us (36%)
  Pallas kernels  28.6 us (32%)
  waiting for transfers between devices  23.8 us (27%)
  local copies, waits for them, and re-layouts  4.18 us (5%)
  between operations  1.02 us (1%)
    ppermute x31, starting transfers between devices, pair_up(): return lax.ppermute(array, 'gz', [(i, i ^ flip) for i in range(groups)])  32 us
    pallas_call x16, Pallas kernels, call(): pl.pallas_call(run, out_shape=out_shape, in_specs=[smem] * len(scalars) +...  28.6 us
    ppermute x31, waiting for transfers between devices, pair_up(): return lax.ppermute(array, 'gz', [(i, i ^ flip) for i in range(groups)])  23.8 us
    unnamed x20, local copies, waits for them, and re-layouts  4.18 us
  transfers between devices with their start and end apart: 31, of which 12 were waited for; matrix products, arithmetic and copies ran while one was open for 0% of the time, Pallas kernels for 28%

profile of v1, /device:TPU:0, one launch (start us, length us, event | category | flops | bytes accessed | tf_op | source)
XLA Modules:
  0.0 89.6 jit_solution(12059602172630255710)
XLA Ops:
  0.6 0.7 copy-done.7
  1.3 0.7 copy-done.9
  2.0 0.6 shard_map.104.refs_3_.refs_4_.refs_7_.refs_6_
  2.5 4.1 %collective-permute-start = (f32[8,256]{1,0:T(8,128)S(1)}, f32[8,256]{1,0:T(8,128)S(1)}, u32[]{:S(2)}, u32[]{:S(2)}) collective-permute-start(f32[8,256]{1,0:T(8,128)S(1)} %shard_map.104.refs_3_.refs_4_.refs_7_.refs_6_), channel_id=1, source_target_pairs={{0,8},{1,9},{2,10},{3,11},{4,12},{5,13},{6,14},{7,15},{8,0},{9,1},... | collective-permute-start | bytes 24584 | tf_op jit(solution)/shard_map/ppermute | solution.py:635
  6.6 0.1 pad_add_fusion.refs_0_
  6.7 1.6 %copy-done = f32[2,2,512,256]{3,2,1,0:T(8,128)S(1)} copy-done((f32[2,2,512,256]{3,2,1,0:T(8,128)S(1)}, f32[2,2,512,256]{3,2,1,0:T(8,128)}, u32[]{:S(2)}) %copy-start) | copy-done | bytes 2097176
  8.3 1.2 %copy-done.3 = bf16[4,512,256]{2,1,0:T(8,128)(2,1)S(1)} copy-done((bf16[4,512,256]{2,1,0:T(8,128)(2,1)S(1)}, bf16[4,512,256]{2,1,0:T(8,128)(2,1)}, u32[]{:S(2)}) %copy-start.3) | copy-done | bytes 1048600
  9.5 1.1 %shard_map.105 = (f32[136,256]{1,0:T(8,128)S(1)}, f32[136,256]{1,0:T(8,128)S(1)}, f32[136,256]{1,0:T(8,128)S(1)}, f32[136,256]{1,0:T(8,128)S(1)}) custom-call(s32[4]{0:T(128)S(1)} %pad_add_fusion.refs_0_, f32[2,2,4,128,256]{4,3,2,1,0:T(8,128)S(1)} %bitcast.5, bf16[4,512,256]{2,1,0:T(8,128)(2,1)S(1)} %copy-done.3, ...), custom_call_target="tpu_custom_call" | custom-call | flops 201326592 | bytes 3702784 | tf_op jit(solution)/shard_map/pallas_call | solution.py:623
  10.7 2.6 %collective-permute-start.6 = (f32[136,256]{1,0:T(8,128)S(1)}, f32[136,256]{1,0:T(8,128)S(1)}, u32[]{:S(2)}, u32[]{:S(2)}) collective-permute-start(f32[136,256]{1,0:T(8,128)S(1)} %get-tuple-element.69), channel_id=1, source_target_pairs={{0,6},{1,7},{2,4},{3,5},{4,2},{5,3},{6,0},{7,1},{8,14},{9,15},{10,... | collective-permute-start | bytes 417800 | tf_op jit(solution)/shard_map/ppermute | solution.py:635
  13.3 0.5 collective-permute-start.2
  13.8 1.1 %shard_map.107 = (f32[136,256]{1,0:T(8,128)S(1)}, f32[136,256]{1,0:T(8,128)S(1)}, f32[136,256]{1,0:T(8,128)S(1)}, f32[136,256]{1,0:T(8,128)S(1)}) custom-call(s32[4]{0:T(128)S(1)} %pad_add_fusion.refs_0_, f32[2,2,4,128,256]{4,3,2,1,0:T(8,128)S(1)} %bitcast.6, bf16[4,512,256]{2,1,0:T(8,128)(2,1)S(1)} %copy-done.3, ...), custom_call_target="tpu_custom_call" | custom-call | flops 201326592 | bytes 3743744 | tf_op jit(solution)/shard_map/pallas_call | solution.py:623
  15.0 0.5 collective-permute-start.4
  15.5 1.1 %shard_map.108 = (f32[136,256]{1,0:T(8,128)S(1)}, f32[136,256]{1,0:T(8,128)S(1)}, f32[136,256]{1,0:T(8,128)S(1)}, f32[136,256]{1,0:T(8,128)S(1)}) custom-call(s32[4]{0:T(128)S(1)} %pad_add_fusion.refs_0_, f32[2,2,4,128,256]{4,3,2,1,0:T(8,128)S(1)} %bitcast.7, bf16[4,512,256]{2,1,0:T(8,128)(2,1)S(1)} %copy-done.3, ...), custom_call_target="tpu_custom_call" | custom-call | flops 201326592 | bytes 3743744 | tf_op jit(solution)/shard_map/pallas_call | solution.py:623
  16.6 0.0 copy-start.2
  16.6 0.0 copy-start.4
  16.6 0.0 copy-start.6
  16.7 0.0 copy-start.8
  16.7 0.9 %collective-permute-start.7 = (f32[136,256]{1,0:T(8,128)S(1)}, f32[136,256]{1,0:T(8,128)S(1)}, u32[]{:S(2)}, u32[]{:S(2)}) collective-permute-start(f32[136,256]{1,0:T(8,128)S(1)} %get-tuple-element.70), channel_id=1, source_target_pairs={{0,7},{1,6},{2,5},{3,4},{4,3},{5,2},{6,1},{7,0},{8,15},{9,14},{10,... | collective-permute-start | bytes 417800 | tf_op jit(solution)/shard_map/ppermute | solution.py:635
  17.6 1.9 %collective-permute-start.3 = (f32[136,256]{1,0:T(8,128)S(1)}, f32[136,256]{1,0:T(8,128)S(1)}, u32[]{:S(2)}, u32[]{:S(2)}) collective-permute-start(f32[136,256]{1,0:T(8,128)S(1)} %get-tuple-element.65.refs_8_), channel_id=1, source_target_pairs={{0,3},{1,2},{2,1},{3,0},{4,7},{5,6},{6,5},{7,4},{8,11},{9,10},{10,... | collective-permute-start | bytes 417800 | tf_op jit(solution)/shard_map/ppermute | solution.py:635
  19.5 1.1 %shard_map.109 = (f32[136,256]{1,0:T(8,128)S(1)}, f32[136,256]{1,0:T(8,128)S(1)}, f32[136,256]{1,0:T(8,128)S(1)}, f32[136,256]{1,0:T(8,128)S(1)}) custom-call(s32[4]{0:T(128)S(1)} %pad_add_fusion.refs_0_, f32[2,2,4,128,256]{4,3,2,1,0:T(8,128)S(1)} %bitcast.8, bf16[4,512,256]{2,1,0:T(8,128)(2,1)S(1)} %copy-done.3, ...), custom_call_target="tpu_custom_call" | custom-call | flops 201326592 | bytes 3743744 | tf_op jit(solution)/shard_map/pallas_call | solution.py:623
  20.6 0.1 collective-permute-start.1
  20.7 0.5 collective-permute-start.5
  21.3 1.5 %collective-permute-start.11 = (f32[136,256]{1,0:T(8,128)S(1)}, f32[136,256]{1,0:T(8,128)S(1)}, u32[]{:S(2)}, u32[]{:S(2)}) collective-permute-start(f32[136,256]{1,0:T(8,128)S(1)} %get-tuple-element.84), channel_id=1, source_target_pairs={{0,2},{1,3},{2,0},{3,1},{4,6},{5,7},{6,4},{7,5},{8,10},{9,11},{10,... | collective-permute-start | bytes 417800 | tf_op jit(solution)/shard_map/ppermute | solution.py:635
  22.8 0.9 %collective-permute-done.7.refs_12_.refs_8_ = f32[136,256]{1,0:T(8,128)S(1)} collective-permute-done((f32[136,256]{1,0:T(8,128)S(1)}, f32[136,256]{1,0:T(8,128)S(1)}, u32[]{:S(2)}, u32[]{:S(2)}) %collective-permute-start.7) | collective-permute-done | bytes 139296 | tf_op jit(solution)/shard_map/ppermute | solution.py:635
  23.7 1.8 %collective-permute-start.15 = (f32[136,256]{1,0:T(8,128)S(1)}, f32[136,256]{1,0:T(8,128)S(1)}, u32[]{:S(2)}, u32[]{:S(2)}) collective-permute-start(f32[136,256]{1,0:T(8,128)S(1)} %get-tuple-element.89), channel_id=1, source_target_pairs={{0,6},{1,7},{2,4},{3,5},{4,2},{5,3},{6,0},{7,1},{8,14},{9,15},{10,... | collective-permute-start | bytes 417800 | tf_op jit(solution)/shard_map/ppermute | solution.py:635
  25.5 0.7 collective-permute-done.3.refs_8_.refs_4_
  26.2 0.1 collective-permute-done.5.refs_10_.refs_6_
  26.2 2.5 %shard_map.110 = (f32[1024,256]{1,0:T(8,128)S(1)}, f32[1024,256]{1,0:T(8,128)S(1)}, f32[6,64,256]{2,1,0:T(8,128)S(1)}, f32[136,256]{1,0:T(8,128)S(1)}, f32[72,256]{1,0:T(8,128)S(1)}, /*index=5*/f32[6]{0:T(128)S(1)}) custom-call(s32[4]{0:T(128)S(1)} %pad_add_fusion.refs_0_, f32[2]{0:T(128)S(1)} %copy-done.8, f32[4,128,256]{2,1,0:T(8,128)S(1)} %copy-done.2, ...), custom_call_target="tpu_custom_call" | custom-call | flops 402653184 | bytes 4612120 | tf_op jit(solution)/shard_map/pallas_call | solution.py:623
  28.7 0.6 collective-permute-start.8
  29.3 1.0 %collective-permute-start.13 = (f32[136,256]{1,0:T(8,128)S(1)}, f32[136,256]{1,0:T(8,128)S(1)}, u32[]{:S(2)}, u32[]{:S(2)}) collective-permute-start(f32[136,256]{1,0:T(8,128)S(1)} %get-tuple-element.86), channel_id=1, source_target_pairs={{0,4},{1,5},{2,6},{3,7},{4,0},{5,1},{6,2},{7,3},{8,12},{9,13},{10,... | collective-permute-start | bytes 417800 | tf_op jit(solution)/shard_map/ppermute | solution.py:635
  30.3 1.1 %collective-permute-start.12 = (f32[136,256]{1,0:T(8,128)S(1)}, f32[136,256]{1,0:T(8,128)S(1)}, u32[]{:S(2)}, u32[]{:S(2)}) collective-permute-start(f32[136,256]{1,0:T(8,128)S(1)} %get-tuple-element.85), channel_id=1, source_target_pairs={{0,3},{1,2},{2,1},{3,0},{4,7},{5,6},{6,5},{7,4},{8,11},{9,10},{10,... | collective-permute-start | bytes 417800 | tf_op jit(solution)/shard_map/ppermute | solution.py:635
  31.4 0.7 shard_map.111.refs_5_.refs_4_
  32.0 0.9 shard_map.112.refs_8_.refs_11_.refs_6_
  33.0 1.2 %collective-permute-start.16 = (f32[136,256]{1,0:T(8,128)S(1)}, f32[136,256]{1,0:T(8,128)S(1)}, u32[]{:S(2)}, u32[]{:S(2)}) collective-permute-start(f32[136,256]{1,0:T(8,128)S(1)} %get-tuple-element.90), channel_id=1, source_target_pairs={{0,7},{1,6},{2,5},{3,4},{4,3},{5,2},{6,1},{7,0},{8,15},{9,14},{10,... | collective-permute-start | bytes 417800 | tf_op jit(solution)/shard_map/ppermute | solution.py:635
  34.2 0.7 collective-permute-start.10
  34.8 1.6 %collective-permute-done.8.refs_10_ = f32[72,256]{1,0:T(8,128)S(1)} collective-permute-done((f32[72,256]{1,0:T(8,128)S(1)}, f32[72,256]{1,0:T(8,128)S(1)}, u32[]{:S(2)}, u32[]{:S(2)}) %collective-permute-start.8) | collective-permute-done | bytes 73760 | tf_op jit(solution)/shard_map/ppermute | solution.py:635
  36.5 5.2 %shard_map.113 = (f32[1024,256]{1,0:T(8,128)S(1)}, f32[1024,256]{1,0:T(8,128)S(1)}, f32[136,256]{1,0:T(8,128)S(1)}, f32[72,256]{1,0:T(8,128)S(1)}) custom-call(s32[4]{0:T(128)S(1)} %pad_add_fusion.refs_0_, f32[6]{0:T(128)S(1)} %get-tuple-element.71.refs_1_, f32[4,128,256]{2,1,0:T(8,128)S(1)} %copy-done.2, bf16[2,256,256]{2,1,0:T(8,128)(2,1)S(1)} %copy-done.4, ...), custom_call_target="tpu_custom_call" | custom-call | flops 855638016 | bytes 7208960 | tf_op jit(solution)/shard_map/pallas_call | solution.py:623
  41.6 1.3 %collective-permute-start.9 = (f32[72,256]{1,0:T(8,128)S(1)}, f32[72,256]{1,0:T(8,128)S(1)}, u32[]{:S(2)}, u32[]{:S(2)}) collective-permute-start(f32[72,256]{1,0:T(8,128)S(1)} %get-tuple-element.80.refs_13_), channel_id=1, source_target_pairs={{0,8},{1,9},{2,10},{3,11},{4,12},{5,13},{6,14},{7,15},{8,0},{9,1},... | collective-permute-start | bytes 221192 | tf_op jit(solution)/shard_map/ppermute | solution.py:635
  42.9 0.4 collective-permute-done.14.refs_10_
  43.4 1.7 %shard_map.114 = (f32[1024,256]{1,0:T(8,128)S(1)}, f32[1024,256]{1,0:T(8,128)S(1)}, f32[6,64,256]{2,1,0:T(8,128)S(1)}, f32[136,256]{1,0:T(8,128)S(1)}, f32[72,256]{1,0:T(8,128)S(1)}) custom-call(s32[4]{0:T(128)S(1)} %pad_add_fusion.refs_0_, f32[6]{0:T(128)S(1)} %get-tuple-element.71.refs_1_, f32[4,128,256]{2,1,0:T(8,128)S(1)} %copy-done.2, ...), custom_call_target="tpu_custom_call" | custom-call | flops 402653184 | bytes 4612096 | tf_op jit(solution)/shard_map/pallas_call | solution.py:623
  45.1 1.4 %collective-permute-start.22 = (f32[72,256]{1,0:T(8,128)S(1)}, f32[72,256]{1,0:T(8,128)S(1)}, u32[]{:S(2)}, u32[]{:S(2)}) collective-permute-start(f32[72,256]{1,0:T(8,128)S(1)} %get-tuple-element.92.refs_5_), channel_id=1, source_target_pairs={{0,8},{1,9},{2,10},{3,11},{4,12},{5,13},{6,14},{7,15},{8,0},{9,1},... | collective-permute-start | bytes 221192 | tf_op jit(solution)/shard_map/ppermute | solution.py:635
  46.4 0.9 shard_map.115.refs_9_.refs_8_.refs_6_
  47.3 1.2 %collective-permute-done.9.refs_8_ = f32[72,256]{1,0:T(8,128)S(1)} collective-permute-done((f32[72,256]{1,0:T(8,128)S(1)}, f32[72,256]{1,0:T(8,128)S(1)}, u32[]{:S(2)}, u32[]{:S(2)}) %collective-permute-start.9) | collective-permute-done | bytes 73760 | tf_op jit(solution)/shard_map/ppermute | solution.py:635
  48.5 1.6 %shard_map.116 = (f32[136,256]{1,0:T(8,128)S(1)}, f32[136,256]{1,0:T(8,128)S(1)}, f32[136,256]{1,0:T(8,128)S(1)}, f32[136,256]{1,0:T(8,128)S(1)}, f32[136,256]{1...) custom-call(s32[4]{0:T(128)S(1)} %pad_add_fusion.refs_0_, ...), custom_call_target="tpu_custom_call" | custom-call | flops 402653184 | bytes 5390336 | tf_op jit(solution)/shard_map/pallas_call | solution.py:623
  50.2 1.3 %collective-permute-start.17 = (f32[136,256]{1,0:T(8,128)S(1)}, f32[136,256]{1,0:T(8,128)S(1)}, u32[]{:S(2)}, u32[]{:S(2)}) collective-permute-start(f32[136,256]{1,0:T(8,128)S(1)} %get-tuple-element.93), channel_id=1, source_target_pairs={{0,6},{1,7},{2,4},{3,5},{4,2},{5,3},{6,0},{7,1},{8,14},{9,15},{10,... | collective-permute-start | bytes 417800 | tf_op jit(solution)/shard_map/ppermute | solution.py:635
  51.4 0.8 collective-permute-start.19
  52.2 2.4 %collective-permute-start.20 = (f32[136,256]{1,0:T(8,128)S(1)}, f32[136,256]{1,0:T(8,128)S(1)}, u32[]{:S(2)}, u32[]{:S(2)}) collective-permute-start(f32[136,256]{1,0:T(8,128)S(1)} %get-tuple-element.96), channel_id=1, source_target_pairs={{0,3},{1,2},{2,1},{3,0},{4,7},{5,6},{6,5},{7,4},{8,11},{9,10},{10,... | collective-permute-start | bytes 417800 | tf_op jit(solution)/shard_map/ppermute | solution.py:635
  54.6 5.2 %shard_map.117 = (f32[1024,256]{1,0:T(8,128)S(1)}, f32[1024,256]{1,0:T(8,128)S(1)}, f32[136,256]{1,0:T(8,128)S(1)}, f32[72,256]{1,0:T(8,128)S(1)}) custom-call(s32[4]{0:T(128)S(1)} %pad_add_fusion.refs_0_, f32[6]{0:T(128)S(1)} %get-tuple-element.71.refs_1_, f32[4,128,256]{2,1,0:T(8,128)S(1)} %copy-done.2, bf16[2,256,256]{2,1,0:T(8,128)(2,1)S(1)} %copy-done.4, ...), custom_call_target="tpu_custom_call" | custom-call | flops 855638016 | bytes 7208960 | tf_op jit(solution)/shard_map/pallas_call | solution.py:623
  59.8 0.5 collective-permute-start.23
  60.3 5.9 %collective-permute-done.23.refs_8_ = f32[72,256]{1,0:T(8,128)S(1)} collective-permute-done((f32[72,256]{1,0:T(8,128)S(1)}, f32[72,256]{1,0:T(8,128)S(1)}, u32[]{:S(2)}, u32[]{:S(2)}) %collective-permute-start.23) | collective-permute-done | bytes 73760 | tf_op jit(solution)/shard_map/ppermute | solution.py:635
  66.2 0.0 copy-start.5
  66.2 1.6 %shard_map.118 = (f32[136,256]{1,0:T(8,128)S(1)}, f32[264,256]{1,0:T(8,128)S(1)}, f32[136,256]{1,0:T(8,128)S(1)}, f32[136,256]{1,0:T(8,128)S(1)}, f32[136,256]{1...) custom-call(s32[4]{0:T(128)S(1)} %pad_add_fusion.refs_0_, ...), custom_call_target="tpu_custom_call" | custom-call | flops 402653184 | bytes 5931008 | tf_op jit(solution)/shard_map/pallas_call | solution.py:623
  67.8 2.4 %collective-permute-start.24 = (f32[136,256]{1,0:T(8,128)S(1)}, f32[136,256]{1,0:T(8,128)S(1)}, u32[]{:S(2)}, u32[]{:S(2)}) collective-permute-start(f32[136,256]{1,0:T(8,128)S(1)} %get-tuple-element.108), channel_id=1, source_target_pairs={{0,6},{1,7},{2,4},{3,5},{4,2},{5,3},{6,0},{7,1},{8,14},{9,15},{10,... | collective-permute-start | bytes 417800 | tf_op jit(solution)/shard_map/ppermute | solution.py:635
  70.3 1.1 %collective-permute-start.25 = (f32[136,256]{1,0:T(8,128)S(1)}, f32[136,256]{1,0:T(8,128)S(1)}, u32[]{:S(2)}, u32[]{:S(2)}) collective-permute-start(f32[136,256]{1,0:T(8,128)S(1)} %get-tuple-element.109), channel_id=1, source_target_pairs={{0,2},{1,3},{2,0},{3,1},{4,6},{5,7},{6,4},{7,5},{8,10},{9,11},{10,... | collective-permute-start | bytes 417800 | tf_op jit(solution)/shard_map/ppermute | solution.py:635
  71.4 0.1 collective-permute-start.30
  71.5 1.1 %collective-permute-done.21.refs_6_ = f32[136,256]{1,0:T(8,128)S(1)} collective-permute-done((f32[136,256]{1,0:T(8,128)S(1)}, f32[136,256]{1,0:T(8,128)S(1)}, u32[]{:S(2)}, u32[]{:S(2)}) %collective-permute-start.21) | collective-permute-done | bytes 139296 | tf_op jit(solution)/shard_map/ppermute | solution.py:635
  72.6 0.9 %collective-permute-start.26 = (f32[136,256]{1,0:T(8,128)S(1)}, f32[136,256]{1,0:T(8,128)S(1)}, u32[]{:S(2)}, u32[]{:S(2)}) collective-permute-start(f32[136,256]{1,0:T(8,128)S(1)} %get-tuple-element.110), channel_id=1, source_target_pairs={{0,7},{1,6},{2,5},{3,4},{4,3},{5,2},{6,1},{7,0},{8,15},{9,14},{10,... | collective-permute-start | bytes 417800 | tf_op jit(solution)/shard_map/ppermute | solution.py:635
  73.6 1.1 %collective-permute-done.24.refs_8_ = f32[136,256]{1,0:T(8,128)S(1)} collective-permute-done((f32[136,256]{1,0:T(8,128)S(1)}, f32[136,256]{1,0:T(8,128)S(1)}, u32[]{:S(2)}, u32[]{:S(2)}) %collective-permute-start.24) | collective-permute-done | bytes 139296 | tf_op jit(solution)/shard_map/ppermute | solution.py:635
  74.7 0.1 collective-permute-start.27
  74.7 2.4 %collective-permute-done.25.refs_9_ = f32[136,256]{1,0:T(8,128)S(1)} collective-permute-done((f32[136,256]{1,0:T(8,128)S(1)}, f32[136,256]{1,0:T(8,128)S(1)}, u32[]{:S(2)}, u32[]{:S(2)}) %collective-permute-start.25) | collective-permute-done | bytes 139296 | tf_op jit(solution)/shard_map/ppermute | solution.py:635
  77.1 0.8 collective-permute-start.28
  77.9 5.7 %collective-permute-done.26.refs_10_ = f32[136,256]{1,0:T(8,128)S(1)} collective-permute-done((f32[136,256]{1,0:T(8,128)S(1)}, f32[136,256]{1,0:T(8,128)S(1)}, u32[]{:S(2)}, u32[]{:S(2)}) %collective-permute-start.26) | collective-permute-done | bytes 139296 | tf_op jit(solution)/shard_map/ppermute | solution.py:635
  83.6 2.6 %collective-permute-done.28.refs_12_ = f32[136,256]{1,0:T(8,128)S(1)} collective-permute-done((f32[136,256]{1,0:T(8,128)S(1)}, f32[136,256]{1,0:T(8,128)S(1)}, u32[]{:S(2)}, u32[]{:S(2)}) %collective-permute-start.28) | collective-permute-done | bytes 139296 | tf_op jit(solution)/shard_map/ppermute | solution.py:635
  86.2 3.3 %shard_map.119 = (f32[2,2,512,256]{3,2,1,0:T(8,128)}, f32[2]{0:T(128)}) custom-call(s32[4]{0:T(128)S(1)} %pad_add_fusion.refs_0_, bf16[4,512,256]{2,1,0:T(8,128)(2,1)S(1)} %copy-done.5, f32[136,256]{1,0:T(8,128)S(1)} %collective-permute-done.17.refs_12_.refs_2_, f32[136,256]{1,0:T(8,128)S(1)} %collective-permute-done.18.refs_13_.refs_3_, ...), custom_call_target="tpu_custom_call" | custom-call | flops 805306368 | bytes 5357576 | tf_op jit(solution)/shard_map/pallas_call | solution.py:623
  (35 shorter events, 0.1 us)
Async XLA Ops:
  0.6 0.7 copy-start.7
  1.3 0.7 copy-start.9
  2.5 8.1 %collective-permute-start = (f32[8,256]{1,0:T(8,128)S(1)}, f32[8,256]{1,0:T(8,128)S(1)}, u32[]{:S(2)}, u32[]{:S(2)}) collective-permute-start(f32[8,256]{1,0:T(8,128)S(1)} %shard_map.104.refs_3_.refs_4_.refs_7_.refs_6_), channel_id=1, source_target_pairs={{0,8},{1,9},{2,10},{3,11},{4,12},{5,13},{6,14},{7,15},{8,0},{9,1},... | collective-permute-start | bytes 24584 | tf_op jit(solution)/shard_map/ppermute | solution.py:635
  6.7 1.6 %copy-start = (f32[2,2,512,256]{3,2,1,0:T(8,128)S(1)}, f32[2,2,512,256]{3,2,1,0:T(8,128)}, u32[]{:S(2)}) copy-start(f32[2,2,512,256]{3,2,1,0:T(8,128)} %param.9) | copy-start | bytes 6291460
  8.3 1.2 %copy-start.3 = (bf16[4,512,256]{2,1,0:T(8,128)(2,1)S(1)}, bf16[4,512,256]{2,1,0:T(8,128)(2,1)}, u32[]{:S(2)}) copy-start(bf16[4,512,256]{2,1,0:T(8,128)(2,1)} %constant.58.clone.refs_2_) | copy-start | bytes 3145732
  9.5 4.3 %copy-start.1 = (f32[2,2,512,256]{3,2,1,0:T(8,128)S(1)}, f32[2,2,512,256]{3,2,1,0:T(8,128)}, u32[]{:S(2)}) copy-start(f32[2,2,512,256]{3,2,1,0:T(8,128)} %param.9) | copy-start | bytes 6291460
  10.7 9.9 %collective-permute-start.6 = (f32[136,256]{1,0:T(8,128)S(1)}, f32[136,256]{1,0:T(8,128)S(1)}, u32[]{:S(2)}, u32[]{:S(2)}) collective-permute-start(f32[136,256]{1,0:T(8,128)S(1)} %get-tuple-element.69), channel_id=1, source_target_pairs={{0,6},{1,7},{2,4},{3,5},{4,2},{5,3},{6,0},{7,1},{8,14},{9,15},{10,... | collective-permute-start | bytes 417800 | tf_op jit(solution)/shard_map/ppermute | solution.py:635
  13.3 7.4 %collective-permute-start.2 = (f32[136,256]{1,0:T(8,128)S(1)}, f32[136,256]{1,0:T(8,128)S(1)}, u32[]{:S(2)}, u32[]{:S(2)}) collective-permute-start(f32[136,256]{1,0:T(8,128)S(1)} %get-tuple-element.63.refs_8_), channel_id=1, source_target_pairs={{0,2},{1,3},{2,0},{3,1},{4,6},{5,7},{6,4},{7,5},{8,10},{9,11},{10,... | collective-permute-start | bytes 417800 | tf_op jit(solution)/shard_map/ppermute | solution.py:635
  15.0 6.3 %collective-permute-start.4 = (f32[136,256]{1,0:T(8,128)S(1)}, f32[136,256]{1,0:T(8,128)S(1)}, u32[]{:S(2)}, u32[]{:S(2)}) collective-permute-start(f32[136,256]{1,0:T(8,128)S(1)} %get-tuple-element.67), channel_id=1, source_target_pairs={{0,4},{1,5},{2,6},{3,7},{4,0},{5,1},{6,2},{7,3},{8,12},{9,13},{10,... | collective-permute-start | bytes 417800 | tf_op jit(solution)/shard_map/ppermute | solution.py:635
  16.6 9.6 %copy-start.2 = (f32[4,128,256]{2,1,0:T(8,128)S(1)}, f32[4,128,256]{2,1,0:T(8,128)}, u32[]{:S(2)}) copy-start(f32[4,128,256]{2,1,0:T(8,128)} %constant.61.clone.refs_2_) | copy-start | bytes 1572868
  16.6 9.6 %copy-start.4 = (bf16[2,256,256]{2,1,0:T(8,128)(2,1)S(1)}, bf16[2,256,256]{2,1,0:T(8,128)(2,1)}, u32[]{:S(2)}) copy-start(bf16[2,256,256]{2,1,0:T(8,128)(2,1)} %constant.60.clone.refs_4_.refs_3_.refs_2_) | copy-start | bytes 786436
  16.6 9.6 %copy-start.6 = (f32[8,256]{1,0:T(8,128)S(1)}, f32[8,256]{1,0:T(8,128)}, u32[]{:S(2)}) copy-start(f32[8,256]{1,0:T(8,128)} %constant.62.clone.refs_3_) | copy-start | bytes 24580
  16.7 9.6 %copy-start.8 = (f32[2]{0:T(128)S(1)}, f32[2]{0:T(128)}, u32[]{:S(2)}) copy-start(f32[2]{0:T(128)} %refs_1_.4) | copy-start | bytes 28
  16.7 7.0 %collective-permute-start.7 = (f32[136,256]{1,0:T(8,128)S(1)}, f32[136,256]{1,0:T(8,128)S(1)}, u32[]{:S(2)}, u32[]{:S(2)}) collective-permute-start(f32[136,256]{1,0:T(8,128)S(1)} %get-tuple-element.70), channel_id=1, source_target_pairs={{0,7},{1,6},{2,5},{3,4},{4,3},{5,2},{6,1},{7,0},{8,15},{9,14},{10,... | collective-permute-start | bytes 417800 | tf_op jit(solution)/shard_map/ppermute | solution.py:635
  17.6 8.6 %collective-permute-start.3 = (f32[136,256]{1,0:T(8,128)S(1)}, f32[136,256]{1,0:T(8,128)S(1)}, u32[]{:S(2)}, u32[]{:S(2)}) collective-permute-start(f32[136,256]{1,0:T(8,128)S(1)} %get-tuple-element.65.refs_8_), channel_id=1, source_target_pairs={{0,3},{1,2},{2,1},{3,0},{4,7},{5,6},{6,5},{7,4},{8,11},{9,10},{10,... | collective-permute-start | bytes 417800 | tf_op jit(solution)/shard_map/ppermute | solution.py:635
  20.6 5.5 %collective-permute-start.1 = (f32[136,256]{1,0:T(8,128)S(1)}, f32[136,256]{1,0:T(8,128)S(1)}, u32[]{:S(2)}, u32[]{:S(2)}) collective-permute-start(f32[136,256]{1,0:T(8,128)S(1)} %get-tuple-element.66), channel_id=1, source_target_pairs={{0,1},{1,0},{2,3},{3,2},{4,5},{5,4},{6,7},{7,6},{8,9},{9,8},{10,11... | collective-permute-start | bytes 417800 | tf_op jit(solution)/shard_map/ppermute | solution.py:635
  20.7 5.5 %collective-permute-start.5 = (f32[136,256]{1,0:T(8,128)S(1)}, f32[136,256]{1,0:T(8,128)S(1)}, u32[]{:S(2)}, u32[]{:S(2)}) collective-permute-start(f32[136,256]{1,0:T(8,128)S(1)} %get-tuple-element.68), channel_id=1, source_target_pairs={{0,5},{1,4},{2,7},{3,6},{4,1},{5,0},{6,3},{7,2},{8,13},{9,12},{10,... | collective-permute-start | bytes 417800 | tf_op jit(solution)/shard_map/ppermute | solution.py:635
  21.3 11.7 %collective-permute-start.11 = (f32[136,256]{1,0:T(8,128)S(1)}, f32[136,256]{1,0:T(8,128)S(1)}, u32[]{:S(2)}, u32[]{:S(2)}) collective-permute-start(f32[136,256]{1,0:T(8,128)S(1)} %get-tuple-element.84), channel_id=1, source_target_pairs={{0,2},{1,3},{2,0},{3,1},{4,6},{5,7},{6,4},{7,5},{8,10},{9,11},{10,... | collective-permute-start | bytes 417800 | tf_op jit(solution)/shard_map/ppermute | solution.py:635
  23.7 10.4 %collective-permute-start.15 = (f32[136,256]{1,0:T(8,128)S(1)}, f32[136,256]{1,0:T(8,128)S(1)}, u32[]{:S(2)}, u32[]{:S(2)}) collective-permute-start(f32[136,256]{1,0:T(8,128)S(1)} %get-tuple-element.89), channel_id=1, source_target_pairs={{0,6},{1,7},{2,4},{3,5},{4,2},{5,3},{6,0},{7,1},{8,14},{9,15},{10,... | collective-permute-start | bytes 417800 | tf_op jit(solution)/shard_map/ppermute | solution.py:635
  28.7 7.7 %collective-permute-start.8 = (f32[72,256]{1,0:T(8,128)S(1)}, f32[72,256]{1,0:T(8,128)S(1)}, u32[]{:S(2)}, u32[]{:S(2)}) collective-permute-start(f32[72,256]{1,0:T(8,128)S(1)} %get-tuple-element.72.refs_9_), channel_id=1, source_target_pairs={{0,8},{1,9},{2,10},{3,11},{4,12},{5,13},{6,14},{7,15},{8,0},{9,1},... | collective-permute-start | bytes 221192 | tf_op jit(solution)/shard_map/ppermute | solution.py:635
  29.3 12.3 %collective-permute-start.13 = (f32[136,256]{1,0:T(8,128)S(1)}, f32[136,256]{1,0:T(8,128)S(1)}, u32[]{:S(2)}, u32[]{:S(2)}) collective-permute-start(f32[136,256]{1,0:T(8,128)S(1)} %get-tuple-element.86), channel_id=1, source_target_pairs={{0,4},{1,5},{2,6},{3,7},{4,0},{5,1},{6,2},{7,3},{8,12},{9,13},{10,... | collective-permute-start | bytes 417800 | tf_op jit(solution)/shard_map/ppermute | solution.py:635
  30.3 12.6 %collective-permute-start.12 = (f32[136,256]{1,0:T(8,128)S(1)}, f32[136,256]{1,0:T(8,128)S(1)}, u32[]{:S(2)}, u32[]{:S(2)}) collective-permute-start(f32[136,256]{1,0:T(8,128)S(1)} %get-tuple-element.85), channel_id=1, source_target_pairs={{0,3},{1,2},{2,1},{3,0},{4,7},{5,6},{6,5},{7,4},{8,11},{9,10},{10,... | collective-permute-start | bytes 417800 | tf_op jit(solution)/shard_map/ppermute | solution.py:635
  33.0 10.0 %collective-permute-start.16 = (f32[136,256]{1,0:T(8,128)S(1)}, f32[136,256]{1,0:T(8,128)S(1)}, u32[]{:S(2)}, u32[]{:S(2)}) collective-permute-start(f32[136,256]{1,0:T(8,128)S(1)} %get-tuple-element.90), channel_id=1, source_target_pairs={{0,7},{1,6},{2,5},{3,4},{4,3},{5,2},{6,1},{7,0},{8,15},{9,14},{10,... | collective-permute-start | bytes 417800 | tf_op jit(solution)/shard_map/ppermute | solution.py:635
  34.2 8.8 %collective-permute-start.10 = (f32[136,256]{1,0:T(8,128)S(1)}, f32[136,256]{1,0:T(8,128)S(1)}, u32[]{:S(2)}, u32[]{:S(2)}) collective-permute-start(f32[136,256]{1,0:T(8,128)S(1)} %get-tuple-element.83), channel_id=1, source_target_pairs={{0,1},{1,0},{2,3},{3,2},{4,5},{5,4},{6,7},{7,6},{8,9},{9,8},{10,11... | collective-permute-start | bytes 417800 | tf_op jit(solution)/shard_map/ppermute | solution.py:635
  36.5 6.9 %collective-permute-start.14 = (f32[136,256]{1,0:T(8,128)S(1)}, f32[136,256]{1,0:T(8,128)S(1)}, u32[]{:S(2)}, u32[]{:S(2)}) collective-permute-start(f32[136,256]{1,0:T(8,128)S(1)} %get-tuple-element.88), channel_id=1, source_target_pairs={{0,5},{1,4},{2,7},{3,6},{4,1},{5,0},{6,3},{7,2},{8,13},{9,12},{10,... | collective-permute-start | bytes 417800 | tf_op jit(solution)/shard_map/ppermute | solution.py:635
  41.6 6.9 %collective-permute-start.9 = (f32[72,256]{1,0:T(8,128)S(1)}, f32[72,256]{1,0:T(8,128)S(1)}, u32[]{:S(2)}, u32[]{:S(2)}) collective-permute-start(f32[72,256]{1,0:T(8,128)S(1)} %get-tuple-element.80.refs_13_), channel_id=1, source_target_pairs={{0,8},{1,9},{2,10},{3,11},{4,12},{5,13},{6,14},{7,15},{8,0},{9,1},... | collective-permute-start | bytes 221192 | tf_op jit(solution)/shard_map/ppermute | solution.py:635
  45.1 9.6 %collective-permute-start.22 = (f32[72,256]{1,0:T(8,128)S(1)}, f32[72,256]{1,0:T(8,128)S(1)}, u32[]{:S(2)}, u32[]{:S(2)}) collective-permute-start(f32[72,256]{1,0:T(8,128)S(1)} %get-tuple-element.92.refs_5_), channel_id=1, source_target_pairs={{0,8},{1,9},{2,10},{3,11},{4,12},{5,13},{6,14},{7,15},{8,0},{9,1},... | collective-permute-start | bytes 221192 | tf_op jit(solution)/shard_map/ppermute | solution.py:635
  50.2 16.0 %collective-permute-start.17 = (f32[136,256]{1,0:T(8,128)S(1)}, f32[136,256]{1,0:T(8,128)S(1)}, u32[]{:S(2)}, u32[]{:S(2)}) collective-permute-start(f32[136,256]{1,0:T(8,128)S(1)} %get-tuple-element.93), channel_id=1, source_target_pairs={{0,6},{1,7},{2,4},{3,5},{4,2},{5,3},{6,0},{7,1},{8,14},{9,15},{10,... | collective-permute-start | bytes 417800 | tf_op jit(solution)/shard_map/ppermute | solution.py:635
  51.4 14.8 %collective-permute-start.18 = (f32[136,256]{1,0:T(8,128)S(1)}, f32[136,256]{1,0:T(8,128)S(1)}, u32[]{:S(2)}, u32[]{:S(2)}) collective-permute-start(f32[136,256]{1,0:T(8,128)S(1)} %get-tuple-element.94), channel_id=1, source_target_pairs={{0,7},{1,6},{2,5},{3,4},{4,3},{5,2},{6,1},{7,0},{8,15},{9,14},{10,... | collective-permute-start | bytes 417800 | tf_op jit(solution)/shard_map/ppermute | solution.py:635
  51.4 20.0 %collective-permute-start.19 = (f32[136,256]{1,0:T(8,128)S(1)}, f32[136,256]{1,0:T(8,128)S(1)}, u32[]{:S(2)}, u32[]{:S(2)}) collective-permute-start(f32[136,256]{1,0:T(8,128)S(1)} %get-tuple-element.95), channel_id=1, source_target_pairs={{0,2},{1,3},{2,0},{3,1},{4,6},{5,7},{6,4},{7,5},{8,10},{9,11},{10,... | collective-permute-start | bytes 417800 | tf_op jit(solution)/shard_map/ppermute | solution.py:635
  52.2 19.2 %collective-permute-start.20 = (f32[136,256]{1,0:T(8,128)S(1)}, f32[136,256]{1,0:T(8,128)S(1)}, u32[]{:S(2)}, u32[]{:S(2)}) collective-permute-start(f32[136,256]{1,0:T(8,128)S(1)} %get-tuple-element.96), channel_id=1, source_target_pairs={{0,3},{1,2},{2,1},{3,0},{4,7},{5,6},{6,5},{7,4},{8,11},{9,10},{10,... | collective-permute-start | bytes 417800 | tf_op jit(solution)/shard_map/ppermute | solution.py:635
  59.8 6.4 %collective-permute-start.23 = (f32[72,256]{1,0:T(8,128)S(1)}, f32[72,256]{1,0:T(8,128)S(1)}, u32[]{:S(2)}, u32[]{:S(2)}) collective-permute-start(f32[72,256]{1,0:T(8,128)S(1)} %get-tuple-element.105.refs_11_), channel_id=1, source_target_pairs={{0,8},{1,9},{2,10},{3,11},{4,12},{5,13},{6,14},{7,15},{8,0},{9,1},... | collective-permute-start | bytes 221192 | tf_op jit(solution)/shard_map/ppermute | solution.py:635
  66.2 6.5 %collective-permute-start.21 = (f32[136,256]{1,0:T(8,128)S(1)}, f32[136,256]{1,0:T(8,128)S(1)}, u32[]{:S(2)}, u32[]{:S(2)}) collective-permute-start(f32[136,256]{1,0:T(8,128)S(1)} %get-tuple-element.97), channel_id=1, source_target_pairs={{0,4},{1,5},{2,6},{3,7},{4,0},{5,1},{6,2},{7,3},{8,12},{9,13},{10,... | collective-permute-start | bytes 417800 | tf_op jit(solution)/shard_map/ppermute | solution.py:635
  66.2 20.0 %copy-start.5 = (bf16[4,512,256]{2,1,0:T(8,128)(2,1)S(1)}, bf16[4,512,256]{2,1,0:T(8,128)(2,1)}, u32[]{:S(2)}) copy-start(bf16[4,512,256]{2,1,0:T(8,128)(2,1)} %constant.59.clone.refs_1_) | copy-start | bytes 3145732
  67.8 6.8 %collective-permute-start.24 = (f32[136,256]{1,0:T(8,128)S(1)}, f32[136,256]{1,0:T(8,128)S(1)}, u32[]{:S(2)}, u32[]{:S(2)}) collective-permute-start(f32[136,256]{1,0:T(8,128)S(1)} %get-tuple-element.108), channel_id=1, source_target_pairs={{0,6},{1,7},{2,4},{3,5},{4,2},{5,3},{6,0},{7,1},{8,14},{9,15},{10,... | collective-permute-start | bytes 417800 | tf_op jit(solution)/shard_map/ppermute | solution.py:635
  70.3 6.9 %collective-permute-start.25 = (f32[136,256]{1,0:T(8,128)S(1)}, f32[136,256]{1,0:T(8,128)S(1)}, u32[]{:S(2)}, u32[]{:S(2)}) collective-permute-start(f32[136,256]{1,0:T(8,128)S(1)} %get-tuple-element.109), channel_id=1, source_target_pairs={{0,2},{1,3},{2,0},{3,1},{4,6},{5,7},{6,4},{7,5},{8,10},{9,11},{10,... | collective-permute-start | bytes 417800 | tf_op jit(solution)/shard_map/ppermute | solution.py:635
  71.4 14.8 %collective-permute-start.29 = (f32[264,256]{1,0:T(8,128)S(1)}, f32[264,256]{1,0:T(8,128)S(1)}, u32[]{:S(2)}, u32[]{:S(2)}) collective-permute-start(f32[264,256]{1,0:T(8,128)S(1)} %get-tuple-element.113), channel_id=1, source_target_pairs={{0,5},{1,4},{2,7},{3,6},{4,1},{5,0},{6,3},{7,2},{8,13},{9,12},{10,... | collective-permute-start | bytes 811016 | tf_op jit(solution)/shard_map/ppermute | solution.py:635
  71.4 14.8 %collective-permute-start.30 = (f32[264,256]{1,0:T(8,128)S(1)}, f32[264,256]{1,0:T(8,128)S(1)}, u32[]{:S(2)}, u32[]{:S(2)}) collective-permute-start(f32[264,256]{1,0:T(8,128)S(1)} %get-tuple-element.114), channel_id=1, source_target_pairs={{0,1},{1,0},{2,3},{3,2},{4,5},{5,4},{6,7},{7,6},{8,9},{9,8},{10,11... | collective-permute-start | bytes 811016 | tf_op jit(solution)/shard_map/ppermute | solution.py:635
  72.6 10.9 %collective-permute-start.26 = (f32[136,256]{1,0:T(8,128)S(1)}, f32[136,256]{1,0:T(8,128)S(1)}, u32[]{:S(2)}, u32[]{:S(2)}) collective-permute-start(f32[136,256]{1,0:T(8,128)S(1)} %get-tuple-element.110), channel_id=1, source_target_pairs={{0,7},{1,6},{2,5},{3,4},{4,3},{5,2},{6,1},{7,0},{8,15},{9,14},{10,... | collective-permute-start | bytes 417800 | tf_op jit(solution)/shard_map/ppermute | solution.py:635
  74.7 8.9 %collective-permute-start.27 = (f32[136,256]{1,0:T(8,128)S(1)}, f32[136,256]{1,0:T(8,128)S(1)}, u32[]{:S(2)}, u32[]{:S(2)}) collective-permute-start(f32[136,256]{1,0:T(8,128)S(1)} %get-tuple-element.111), channel_id=1, source_target_pairs={{0,3},{1,2},{2,1},{3,0},{4,7},{5,6},{6,5},{7,4},{8,11},{9,10},{10,... | collective-permute-start | bytes 417800 | tf_op jit(solution)/shard_map/ppermute | solution.py:635
  77.1 9.0 %collective-permute-start.28 = (f32[136,256]{1,0:T(8,128)S(1)}, f32[136,256]{1,0:T(8,128)S(1)}, u32[]{:S(2)}, u32[]{:S(2)}) collective-permute-start(f32[136,256]{1,0:T(8,128)S(1)} %get-tuple-element.112), channel_id=1, source_target_pairs={{0,4},{1,5},{2,6},{3,7},{4,0},{5,1},{6,2},{7,3},{8,12},{9,13},{10,... | collective-permute-start | bytes 417800 | tf_op jit(solution)/shard_map/ppermute | solution.py:635
